TPU v7x, 32 devices: a whole 2x2x4 slice. The times are simulated.
32 devices in a mesh: section: 4 (over y, core), tp: 4 (over z), rep: 2 (over x).
Axes of the slice: x: 2, y: 2, z: 4, core: 2. Of those that a mesh axis runs over, the one named last changes fastest.
Arguments:
- student_noise: float32 [2, 768, 64], P('rep', 'section'), may hold values from -10 to 10
- renoise_noise: float32 [2, 768, 64], P('rep', 'section'), may hold values from -10 to 10
- patch_slot: int32 [2, 768], P('rep', 'section'), may hold values from 0 to 767, each once within a row
- renoise_step: int32 [2], P('rep'), may hold values from 20 to 979
- prompt_ids: int32 [2, 256], P('rep'), may hold values from 0 to 31999
- text_table: bfloat16 [32000, 2432], P(('section', 'tp')), may hold values from -48 to 48
- student_in: bfloat16 [64, 2432], replicated, may hold values from -0.75 to 0.75
- student_qkv: bfloat16 [2432, 3, 2048], P('section', None, 'tp'), may hold values from -2 to 2
- student_out: bfloat16 [2432, 2048], P('section', 'tp'), may hold values from -0.375 to 0.375
- student_final: bfloat16 [2432, 64], replicated, may hold values from -0.125 to 0.125
- real_in: bfloat16 [64, 2432], replicated, may hold values from -0.75 to 0.75
- real_qkv: bfloat16 [2432, 3, 2048], P('section', None, 'tp'), may hold values from -2 to 2
- real_out: bfloat16 [2432, 2048], P('section', 'tp'), may hold values from -0.375 to 0.375
- real_final: bfloat16 [2432, 64], replicated, may hold values from -0.125 to 0.125
- fake_in: bfloat16 [64, 2432], replicated, may hold values from -0.75 to 0.75
- fake_qkv: bfloat16 [2432, 3, 2048], P('section', None, 'tp'), may hold values from -2 to 2
- fake_out: bfloat16 [2432, 2048], P('section', 'tp'), may hold values from -0.375 to 0.375
- fake_final: bfloat16 [2432, 64], replicated, may hold values from -0.125 to 0.125
Outputs:
- latent_grad: float32 [2, 768, 64], P('rep', 'section')
All inputs are finite; a program needn't handle non-finite values. Where the computation divides by a largest or mean magnitude, that divisor is 1e-20 or more.
Results may differ from a plain program's by a relative error of at most 0.03.
Values may be sent and summed in bfloat16 or wider, within the bound.
A program may use at most 128 MiB of HBM per device.

v0:
```python
import math

import jax
import jax.numpy as jnp
from jax import lax
from jax.sharding import PartitionSpec as P

D = 2432
HD = 64
GRID_W = 64


def time_embed(step_time):
    half_width = D // 2
    frequency = jnp.exp(-math.log(10000.0) * jnp.arange(half_width, dtype=jnp.float32) / half_width)
    angles = 1000.0 * step_time * frequency
    return jnp.concatenate([jnp.cos(angles), jnp.sin(angles)])


def place_embed(slots):
    quarter = D // 4
    frequency = jnp.exp(-math.log(10000.0) * jnp.arange(quarter, dtype=jnp.float32) / quarter)
    row_angle = (slots // GRID_W).astype(jnp.float32)[:, None] * frequency[None, :]
    col_angle = (slots % GRID_W).astype(jnp.float32)[:, None] * frequency[None, :]
    return jnp.concatenate(
        [jnp.sin(row_angle), jnp.cos(row_angle), jnp.sin(col_angle), jnp.cos(col_angle)], axis=1
    )


def rms_norm(values):
    return values * lax.rsqrt(jnp.mean(values * values, axis=-1, keepdims=True) + 1e-06)


def final_layer(after, w_final):
    return jnp.einsum(
        "ntd,ndc->ntc",
        rms_norm(after).astype(jnp.bfloat16),
        w_final,
        preferred_element_type=jnp.float32,
    )


def networks(latents, step_times, condition, w_in, w_qkv, w_out, w_final):
    count = latents.shape[0]
    tok_local = latents.shape[1]
    head_cols = w_out.shape[2]
    local_heads = head_cols // HD
    hidden = jnp.einsum(
        "ntc,ncd->ntd", latents.astype(jnp.bfloat16), w_in, preferred_element_type=jnp.float32
    )
    hidden = hidden + condition[None, :, :] + jax.vmap(time_embed)(step_times)[:, None, :]
    normed = rms_norm(hidden).astype(jnp.bfloat16)
    projected = jnp.einsum(
        "ntd,dnkc->ntkc",
        normed,
        lax.all_gather(w_qkv, "section", axis=0, tiled=True),
        preferred_element_type=jnp.float32,
    )
    projected = projected.astype(jnp.bfloat16)
    queries = projected[:, :, 0].reshape(count, tok_local, local_heads, HD)
    keys_local = projected[:, :, 1]
    values_local = projected[:, :, 2]
    row_max = jnp.full((count, local_heads, tok_local), -1e30, jnp.float32)
    key_block = lax.all_gather(keys_local, "section", axis=1, tiled=True)
    value_block = lax.all_gather(values_local, "section", axis=1, tiled=True)
    key_count = key_block.shape[1]
    key_heads = key_block.reshape(count, key_count, local_heads, HD)
    value_heads = value_block.reshape(count, key_count, local_heads, HD)
    scores = jnp.einsum(
        "nqhd,nkhd->nhqk", queries, key_heads, preferred_element_type=jnp.float32
    ) * HD ** (-0.5)
    new_max = jnp.maximum(row_max, jnp.max(scores, axis=3))
    expo = jnp.exp(scores - new_max[..., None])
    totals = jnp.sum(expo, axis=3)
    running = jnp.einsum(
        "nhqk,nkhd->nhqd",
        expo.astype(jnp.bfloat16),
        value_heads,
        preferred_element_type=jnp.float32,
    )
    row_max, totals, running = (new_max, totals, running)
    mixed = (running / totals[..., None]).astype(jnp.bfloat16)
    mixed = mixed.transpose(0, 2, 1, 3).reshape(count, tok_local, head_cols)
    group_terms = jnp.einsum(
        "ntc,rnc->ntr",
        mixed,
        lax.all_gather(w_out, "section", axis=0, tiled=True),
        preferred_element_type=jnp.float32,
    )
    attended = lax.psum(group_terms.astype(jnp.bfloat16), "tp").astype(jnp.float32)
    return final_layer(hidden + attended, w_final)


def per_device(
    student_noise,
    renoise_noise,
    patch_slot,
    renoise_step,
    prompt_ids,
    text_table,
    student_in,
    student_qkv,
    student_out,
    student_final,
    real_in,
    real_qkv,
    real_out,
    real_final,
    fake_in,
    fake_qkv,
    fake_out,
    fake_final,
):
    vocab_local = text_table.shape[0]
    first_row = lax.axis_index(("section", "tp")) * vocab_local
    prompt_row = prompt_ids[0] - first_row
    matches = (prompt_row[:, None] == jnp.arange(vocab_local, dtype=jnp.int32)[None, :]).astype(
        jnp.bfloat16
    )
    counts = jnp.sum(matches.astype(jnp.float32), axis=0).astype(jnp.bfloat16)
    partial_pool = jnp.dot(counts, text_table, preferred_element_type=jnp.float32)
    pooled = lax.psum(partial_pool, ("section", "tp")) / prompt_ids.shape[1]
    condition = place_embed(patch_slot[0]) + pooled[None, :]
    start_noise = student_noise[0]
    velocity = networks(
        start_noise[None],
        jnp.ones((1,), jnp.float32),
        condition,
        student_in[None],
        student_qkv[:, None],
        student_out[:, None],
        student_final[None],
    )[0]
    clean = start_noise - velocity
    step_time = renoise_step[0].astype(jnp.float32) / 1000.0
    noisy = (1.0 - step_time) * clean + step_time * renoise_noise[0]
    step_row = jnp.full((1,), step_time, jnp.float32)
    real_velocity = networks(
        noisy[None],
        step_row,
        condition,
        real_in[None],
        real_qkv[:, None],
        real_out[:, None],
        real_final[None],
    )[0]
    fake_velocity = networks(
        noisy[None],
        step_row,
        condition,
        fake_in[None],
        fake_qkv[:, None],
        fake_out[:, None],
        fake_final[None],
    )[0]
    pred_real = noisy - step_time * real_velocity
    pred_fake = noisy - step_time * fake_velocity
    local_spread = jnp.sum(jnp.abs(clean - pred_real))
    entries = noisy.shape[0] * lax.axis_size("section") * noisy.shape[1]
    spread = lax.psum(local_spread, "section") / entries + 1e-05
    return ((pred_fake - pred_real) / spread)[None]


def solution(mesh):
    placed = (
        P("rep", "section", None),
        P("rep", "section", None),
        P("rep", "section"),
        P("rep"),
        P("rep", None),
        P(("section", "tp"), None),
        P(),
        P("section", None, "tp"),
        P("section", "tp"),
        P(),
        P(),
        P("section", None, "tp"),
        P("section", "tp"),
        P(),
        P(),
        P("section", None, "tp"),
        P("section", "tp"),
        P(),
    )
    return jax.shard_map(
        per_device, mesh=mesh, in_specs=placed, out_specs=P("rep", "section", None), check_vma=False
    )
```

profile of v0, /device:TPU:0, one launch (start us, length us, event | category | flops | bytes accessed | tf_op | source)
XLA Modules:
  0.0 443.6 jit_solution(9272723195576389616)
XLA Ops:
  6.5 0.7 all-gather.19.cloned.1.call-update
  7.3 0.7 all-gather.21.cloned.1.call-update
  8.5 5.1 %convolution_reduce_fusion = f32[2432]{0:T(1024)S(1)} fusion(bf16[2000,1]{0,1:T(2,128)(2,1)S(1)} %reshape.467, bf16[2000,2432]{1,0:T(8,128)(2,1)} %param.23), kind=kOutput, calls=%fused_computation.62 | convolution fusion | flops 9728000 | bytes 9741728 | tf_op jit(solution)/shard_map/dot_general | solution.py:121
  13.7 4.5 %multiply_cosine_fusion = (f32[192,608]{1,0:T(8,128)S(1)}, f32[192,608]{1,0:T(8,128)S(1)}, f32[192,608]{1,0:T(8,128)}, f32[192,608]{1,0:T(8,128)}) fusion(f32[192]{0:T(256)S(1)} %get-tuple-element.22, f32[608]{0:T(1024)S(1)} %multiply_exponential_fusion.1, f32[192]{0:T(256)S(1)} %get-tuple-element.23), kind=kLoop, calls=%fused_computation.83 | loop fusion | flops 233472 | bytes 1871744 | tf_op jit(solution)/shard_map/cos | solution.py:26
  18.1 2.0 concatenate.10
  20.4 64.6 %psum.35 = f32[2432]{0:T(1024)S(1)} all-reduce(f32[2432]{0:T(1024)S(1)} %convolution_reduce_fusion), channel_id=1, replica_groups=mesh['section'=4,'tp'=4,'rep'=2] {'section','tp'}, use_global_device_ids=true, to_apply=%region_1.0 | all-reduce | flops 2432 | bytes 19456 | tf_op jit(solution)/shard_map/psum | solution.py:122
  84.9 1.8 multiply_reduce_fusion.8
  86.7 5.5 %fusion.25 = bf16[1,192,3,512]{3,1,2,0:T(8,128)(2,1)S(1)} fusion(bf16[2432,3,512]{2,0,1:T(8,128)(2,1)} %all-gather.19.cloned.1.call-done, f32[192,2432]{1,0:T(8,128)} %get-tuple-element.25, f32[192]{0:T(256)S(1)} %add_rsqrt_fusion.5), kind=kOutput, calls=%fused_computation.53 | convolution fusion | flops 1435680768 | bytes 9929472 | tf_op jit(solution)/shard_map/ntd,dnkc->ntkc/dot_general | solution.py:53
  92.3 7.6 %all-gather.1 = bf16[1,768,1,512]{3,1,2,0:T(8,128)(2,1)S(1)} all-gather(bf16[1,192,1,512]{3,1,2,0:T(8,128)(2,1)S(1)} %get-tuple-element.13), channel_id=3, replica_groups=mesh['section'=4,'tp'=4,'rep'=2] {'section'}, dimensions={1}, use_global_device_ids=true | all-gather | bytes 983040 | tf_op jit(solution)/shard_map/all_gather | solution.py:64
  99.9 1.2 copy.38
  101.2 8.7 %all-gather.2 = bf16[1,768,1,512]{3,1,2,0:T(8,128)(2,1)S(1)} all-gather(bf16[1,192,1,512]{3,1,2,0:T(8,128)(2,1)S(1)} %get-tuple-element.14), channel_id=4, replica_groups=mesh['section'=4,'tp'=4,'rep'=2] {'section'}, dimensions={1}, use_global_device_ids=true | all-gather | bytes 983040 | tf_op jit(solution)/shard_map/all_gather | solution.py:65
  109.9 1.2 copy.39
  111.1 2.0 multiply_reduce_fusion.2
  113.1 1.0 fusion.3
  114.3 1.1 fusion.36
  115.4 3.6 fusion.9
  122.7 43.3 %all-reduce.4.cloned.1.call-done = bf16[1,192,2432]{2,1,0:T(8,128)(2,1)} async-done(((bf16[1,192,2432]{2,1,0:T(8,128)(2,1)}), bf16[1,192,2432]{2,1,0:T(8,128)(2,1)}) %all-reduce.4.cloned.1.call-update) | async-done | bytes 933904 | tf_op jit(solution)/shard_map/psum | solution.py:90
  166.0 2.3 multiply_reduce_fusion.7
  168.6 1.1 fusion.75
  169.8 1.8 multiply_reduce_fusion.4
  171.6 48.4 %all-gather.27.cloned.1.call-done = bf16[2432,3,512]{2,0,1:T(8,128)(2,1)} async-done(((bf16[608,3,512]{2,0,1:T(8,128)(2,1)}), bf16[2432,3,512]{2,0,1:T(8,128)(2,1)}) %all-gather.27.cloned.1.call-update) | async-done | bytes 7471120 | tf_op jit(solution)/shard_map/all_gather | solution.py:56
  219.9 5.4 %fusion.27 = bf16[1,192,3,512]{3,1,2,0:T(8,128)(2,1)S(1)} fusion(bf16[2432,3,512]{2,0,1:T(8,128)(2,1)} %all-gather.27.cloned.1.call-done, f32[192,2432]{1,0:T(8,128)} %get-tuple-element.33, f32[192]{0:T(256)S(1)} %add_rsqrt_fusion.1), kind=kOutput, calls=%fused_computation.55 | convolution fusion | flops 1435680768 | bytes 9929472 | tf_op jit(solution)/shard_map/ntd,dnkc->ntkc/dot_general | solution.py:53
  225.4 0.7 fusion.93
  226.1 10.2 %all-gather.9 = bf16[1,768,1,512]{3,1,2,0:T(8,128)(2,1)S(1)} all-gather(bf16[1,192,1,512]{3,1,2,0:T(8,128)(2,1)S(1)} %get-tuple-element.7), channel_id=11, replica_groups=mesh['section'=4,'tp'=4,'rep'=2] {'section'}, dimensions={1}, use_global_device_ids=true | all-gather | bytes 983040 | tf_op jit(solution)/shard_map/all_gather | solution.py:64
  236.3 1.2 copy.44
  237.6 13.5 %all-gather.10 = bf16[1,768,1,512]{3,1,2,0:T(8,128)(2,1)S(1)} all-gather(bf16[1,192,1,512]{3,1,2,0:T(8,128)(2,1)} %get-tuple-element.8), channel_id=12, replica_groups=mesh['section'=4,'tp'=4,'rep'=2] {'section'}, dimensions={1}, use_global_device_ids=true | all-gather | bytes 983040 | tf_op jit(solution)/shard_map/all_gather | solution.py:65
  251.1 1.2 copy.45
  252.3 2.8 multiply_reduce_fusion.6
  255.1 24.7 %all-gather.23.cloned.1.call-done = bf16[2432,3,512]{2,0,1:T(8,128)(2,1)} async-done(((bf16[608,3,512]{2,0,1:T(8,128)(2,1)}), bf16[2432,3,512]{2,0,1:T(8,128)(2,1)}) %all-gather.23.cloned.1.call-update) | async-done | bytes 7471120 | tf_op jit(solution)/shard_map/all_gather | solution.py:56
  279.8 5.4 %fusion.26 = bf16[1,192,3,512]{3,1,2,0:T(8,128)(2,1)S(1)} fusion(bf16[2432,3,512]{2,0,1:T(8,128)(2,1)} %all-gather.23.cloned.1.call-done, f32[192,2432]{1,0:T(8,128)} %get-tuple-element.31, f32[192]{0:T(256)S(1)} %add_rsqrt_fusion.3), kind=kOutput, calls=%fused_computation.54 | convolution fusion | flops 1435680768 | bytes 9929472 | tf_op jit(solution)/shard_map/ntd,dnkc->ntkc/dot_general | solution.py:53
  285.2 0.7 fusion.94
  286.0 11.7 %all-gather.5 = bf16[1,768,1,512]{3,1,2,0:T(8,128)(2,1)S(1)} all-gather(bf16[1,192,1,512]{3,1,2,0:T(8,128)(2,1)S(1)} %get-tuple-element.10), channel_id=7, replica_groups=mesh['section'=4,'tp'=4,'rep'=2] {'section'}, dimensions={1}, use_global_device_ids=true | all-gather | bytes 983040 | tf_op jit(solution)/shard_map/all_gather | solution.py:64
  298.1 13.7 %all-gather.6 = bf16[1,768,1,512]{3,1,2,0:T(8,128)(2,1)S(1)} all-gather(bf16[1,192,1,512]{3,1,2,0:T(8,128)(2,1)} %get-tuple-element.11), channel_id=8, replica_groups=mesh['section'=4,'tp'=4,'rep'=2] {'section'}, dimensions={1}, use_global_device_ids=true | all-gather | bytes 983040 | tf_op jit(solution)/shard_map/all_gather | solution.py:65
  311.8 1.2 copy.42
  313.0 0.9 multiply_reduce_fusion
  313.9 3.0 multiply_reduce_fusion.1
  316.9 1.0 fusion.7
  318.0 1.1 fusion.48
  319.2 3.9 fusion.11
  323.1 3.4 fusion.5
  326.6 1.1 fusion.42
  327.7 11.6 %all-gather.25.cloned.1.call-done = bf16[2432,512]{1,0:T(8,128)(2,1)} async-done(((bf16[608,512]{1,0:T(8,128)(2,1)}), bf16[2432,512]{1,0:T(8,128)(2,1)}) %all-gather.25.cloned.1.call-update) | async-done | bytes 2490384 | tf_op jit(solution)/shard_map/all_gather | solution.py:87
  339.3 3.7 fusion.10
  343.0 79.3 %all-reduce.6.cloned.1.call-done = (bf16[1,192,2432]{2,1,0:T(8,128)(2,1)}, bf16[1,192,2432]{2,1,0:T(8,128)(2,1)}) async-done(((bf16[1,192,2432]{2,1,0:T(8,128)(2,1)}, bf16[1,192,2432]{2,1,0:T(8,128)(2,1)}), (bf16[1,192,2432]{2,1,0:T(8,128)(2,1)}, bf16[1,192,2432]{2,1,0:T(8,128)(2,1)})) %all-reduce.6.cloned.1.call-update) | async-done | bytes 1867792 | tf_op jit(solution)/shard_map/psum | solution.py:90
  422.3 1.7 multiply_reduce_fusion.3
  424.3 1.8 fusion.73
  426.2 7.2 %psum.39 = f32[]{:T(128)} all-reduce(f32[]{:T(128)} %get-tuple-element.38), channel_id=1, replica_groups=mesh['section'=4,'tp'=4,'rep'=2] {'section'}, use_global_device_ids=true, to_apply=%region_18.19 | all-reduce | flops 1 | bytes 8 | tf_op jit(solution)/shard_map/psum | solution.py:160
  435.0 1.8 fusion.31
  (93 shorter events, 6.2 us)
Async XLA Ops:
  6.5 78.4 %copy-start = (bf16[64,2432]{1,0:T(8,128)(2,1)S(1)}, bf16[64,2432]{1,0:T(8,128)(2,1)}, u32[]{:S(2)}) copy-start(bf16[64,2432]{1,0:T(8,128)(2,1)} %param.24) | copy-start | bytes 933892
  6.5 1.5 copy-start.21
  6.5 1.6 copy-start.22
  6.5 80.2 %all-gather.19.cloned.1.call-start = ((), (), s32[]{:S(2)}) async-start(), calls=%async_computation.1 | async-start | bytes 9338880 | tf_op jit(solution)/shard_map/all_gather | solution.py:56
  7.3 108.1 %all-gather.21.cloned.1.call-start = ((), (), s32[]{:S(2)}) async-start(), calls=%async_computation.2 | async-start | bytes 3112960 | tf_op jit(solution)/shard_map/all_gather | solution.py:87
  8.0 158.0 %all-reduce.4.cloned.1.call-start = ((), (), s32[]{:S(2)}) async-start(), calls=%async_computation | async-start | bytes 1867776 | tf_op jit(solution)/shard_map/psum | solution.py:90
  18.1 66.8 %copy-start.13 = (f32[1,192,64]{1,2,0:T(8,128)S(1)}, f32[1,192,64]{1,2,0:T(8,128)}, u32[]{:S(2)}) copy-start(f32[1,192,64]{1,2,0:T(8,128)} %param.18) | copy-start | bytes 147460
  113.1 1.1 copy-start.12
  119.0 100.9 %all-gather.27.cloned.1.call-start = ((), (), s32[]{:S(2)}) async-start(), calls=%async_computation.5 | async-start | bytes 9338880 | tf_op jit(solution)/shard_map/all_gather | solution.py:56
  119.6 160.2 %all-gather.23.cloned.1.call-start = ((), (), s32[]{:S(2)}) async-start(), calls=%async_computation.3 | async-start | bytes 9338880 | tf_op jit(solution)/shard_map/all_gather | solution.py:56
  120.2 48.1 %copy-start.15 = (bf16[2432,64]{0,1:T(8,128)(2,1)S(1)}, bf16[2432,64]{0,1:T(8,128)(2,1)}, u32[]{:S(2)}) copy-start(bf16[2432,64]{0,1:T(8,128)(2,1)} %param.27) | copy-start | bytes 933892
  120.2 48.1 %copy-start.18 = (f32[1,192,64]{1,2,0:T(8,128)S(1)}, f32[1,192,64]{1,2,0:T(8,128)}, u32[]{:S(2)}) copy-start(f32[1,192,64]{1,2,0:T(8,128)} %param.19) | copy-start | bytes 147460
  120.2 198.9 %all-gather.29.cloned.1.call-start = ((), (), s32[]{:S(2)}) async-start(), calls=%async_computation.6 | async-start | bytes 3112960 | tf_op jit(solution)/shard_map/all_gather | solution.py:87
  120.8 218.5 %all-gather.25.cloned.1.call-start = ((), (), s32[]{:S(2)}) async-start(), calls=%async_computation.4 | async-start | bytes 3112960 | tf_op jit(solution)/shard_map/all_gather | solution.py:87
  121.6 300.7 %all-reduce.6.cloned.1.call-start = ((), (), s32[]{:S(2)}) async-start(), calls=%async_computation.7 | async-start | bytes 3735552 | tf_op jit(solution)/shard_map/psum | solution.py:90
  166.0 2.4 copy-start.2
  166.0 2.6 copy-start.6
  168.3 1.5 copy-start.14
  297.7 15.3 %copy-start.9 = (bf16[1,768,1,512]{1,3,2,0:T(8,128)(2,1)S(1)}, bf16[1,768,1,512]{1,3,2,0:T(8,128)(2,1)}, u32[]{:S(2)}) copy-start(bf16[1,768,1,512]{1,3,2,0:T(8,128)(2,1)} %copy.44) | copy-start | bytes 2359300
  316.9 1.1 copy-start.10
  318.0 8.5 %slice-start = ((s8[4718592]{0:T(1024)(128)(4,1)}), s8[524288]{0:T(1024)(128)(4,1)S(1)}, s32[]{:S(2)}) async-start(s8[4718592]{0:T(1024)(128)(4,1)} %bitcast.164), calls=%async_computation.8 | async-start | bytes 1048576
  319.2 7.4 %slice-start.1 = ((s8[4718592]{0:T(1024)(128)(4,1)}), s8[4194304]{0:T(1024)(128)(4,1)S(1)}, s32[]{:S(2)}) async-start(s8[4718592]{0:T(1024)(128)(4,1)} %bitcast.164), calls=%async_computation.9 | async-start | bytes 8388608
  323.1 3.4 copy-start.11
  339.3 83.0 %copy-start.4 = (f32[192,2432]{1,0:T(8,128)S(1)}, f32[192,2432]{1,0:T(8,128)}, u32[]{:S(2)}) copy-start(f32[192,2432]{1,0:T(8,128)} %get-tuple-element.33) | copy-start | bytes 5603332
  343.0 81.0 %copy-start.16 = (bf16[2432,64]{0,1:T(8,128)(2,1)S(1)}, bf16[2432,64]{0,1:T(8,128)(2,1)}, u32[]{:S(2)}) copy-start(bf16[2432,64]{0,1:T(8,128)(2,1)} %param.31) | copy-start | bytes 933892
  343.0 81.0 %copy-start.19 = (f32[192,64]{0,1:T(8,128)S(1)}, f32[192,64]{0,1:T(8,128)}, u32[]{:S(2)}) copy-start(f32[192,64]{0,1:T(8,128)} %get-tuple-element.29) | copy-start | bytes 147460
  422.3 1.8 copy-start.5
  422.3 2.0 copy-start.8
  424.0 9.4 %copy-start.3 = (f32[192,2432]{1,0:T(8,128)S(1)}, f32[192,2432]{1,0:T(8,128)}, u32[]{:S(2)}) copy-start(f32[192,2432]{1,0:T(8,128)} %get-tuple-element.31) | copy-start | bytes 5603332
  424.0 9.4 %copy-start.7 = (bf16[1,192,2432]{2,1,0:T(8,128)(2,1)S(1)}, bf16[1,192,2432]{2,1,0:T(8,128)(2,1)}, u32[]{:S(2)}) copy-start(bf16[1,192,2432]{2,1,0:T(8,128)(2,1)} %get-tuple-element.5) | copy-start | bytes 2801668
  426.2 8.8 %copy-start.17 = (bf16[2432,64]{0,1:T(8,128)(2,1)S(1)}, bf16[2432,64]{0,1:T(8,128)(2,1)}, u32[]{:S(2)}) copy-start(bf16[2432,64]{0,1:T(8,128)(2,1)} %param.35) | copy-start | bytes 933892
  426.2 8.8 %copy-start.20 = (f32[192,64]{0,1:T(8,128)S(1)}, f32[192,64]{0,1:T(8,128)}, u32[]{:S(2)}) copy-start(f32[192,64]{0,1:T(8,128)} %get-tuple-element.39) | copy-start | bytes 147460
  433.3 3.5 copy-start.1
Sparse Core Ops, SparseCore 0:
  8.9 56.1 all-gather.18
  66.7 24.9 all-gather.20
  119.2 46.8 all-reduce.3
  167.5 52.3 all-gather.26
  221.4 58.3 all-gather.22
  281.3 31.4 all-gather.28
  314.4 24.7 all-gather.24
  343.2 79.0 all-reduce.5
where the time goes:
time: 444 us
  waiting for transfers between devices  211 us (48%)
  blocking collectives  137 us (31%)
  matrix products  53.1 us (12%)
  other arithmetic  15.8 us (4%)
  between operations  15.2 us (3%)
  local copies, waits for them, and re-layouts  10.8 us (2%)
    psum x2, waiting for transfers between devices, networks(): lax.psum(group_terms.astype(jnp.bfloat16), 'tp').astype(jnp.float32)  123 us
    all_gather x3, waiting for transfers between devices, networks(): lax.all_gather(w_qkv, 'section', axis=0, tiled=True)  73.1 us
    psum x1, blocking collectives, per_device(): pooled = lax.psum(partial_pool, ('section', 'tp')) / prompt_ids.shape[1]  64.6 us
    all_gather x3, blocking collectives, networks(): value_block = lax.all_gather(values_local, 'section', axis=1, tiled=True)  36 us
    all_gather x3, blocking collectives, networks(): key_block = lax.all_gather(keys_local, 'section', axis=1, tiled=True)  29.5 us
    dot_general x3, matrix products, networks(): jnp.einsum('ntd,dnkc->ntkc', normed, lax.all_gather(w_qkv, 'section', axi...  16.3 us
    all_gather x3, waiting for transfers between devices, networks(): lax.all_gather(w_out, 'section', axis=0, tiled=True)  11.6 us
    dot_general x3, matrix products, networks(): jnp.einsum('ntc,rnc->ntr', mixed, lax.all_gather(w_out, 'section', axis=0...  11.3 us
  transfers between devices with their start and end apart: 8, of which 5 were waited for; matrix products, arithmetic and copies ran while one was open for 15% of the time, Pallas kernels for 0%

commit v1 on v0

--- a/solution.py
+++ b/solution.py
@@ -3,6 +3,8 @@
 import jax
 import jax.numpy as jnp
 from jax import lax
+from jax.experimental import pallas as pl
+from jax.experimental.pallas import tpu as pltpu
 from jax.sharding import PartitionSpec as P
 
 D = 2432
@@ -161,6 +163,359 @@
     return ((pred_fake - pred_real) / spread)[None]
 
 
+MESH = pl.DeviceIdType.MESH
+NETS = 3
+
+
+def dot(a, b):
+    return jnp.dot(a, b, preferred_element_type=jnp.float32)
+
+
+def step_kernel(
+    pool_ref, pack_ref, noise_ref, table_ref, time_ref, when_ref, win_ref, fin_ref,
+    wq0_ref, wq1_ref, wq2_ref, wo0_ref, wo1_ref, wo2_ref,
+    out_ref,
+    pool_sum, pool_sec, pool_tp, pack_all, noise_all, row_hot, col_hot, zin, cond, hid, normed,
+    far_send, far_recv, cross_send, cross_recv, near_send, near_recv, own, qkv,
+    mix, z_send, z_recv, z_own, f_mine, f_sib, f_pair, f_cross, f_pack, flow, clean, noisy,
+    send_sem, recv_sem,
+):
+    wq = (wq0_ref, wq1_ref, wq2_ref)
+    wo = (wo0_ref, wo1_ref, wo2_ref)
+    sec = lax.axis_index("section")
+    tp = lax.axis_index("tp")
+    core = lax.rem(sec, 2)
+    sib = sec + 1 - 2 * core
+    cross = lax.rem(sec + 2, 4)
+    diag = lax.rem(sib + 2, 4)
+    tok = pack_ref.shape[0]
+    total = 4 * tok
+    feat = hid.shape[2]
+    half = total // 2
+    chunks = ((0, half), (half, half))
+    tile = tok
+    counter = [0]
+    sends = []
+
+    def send(src, dst, where):
+        at = counter[0]
+        counter[0] += 1
+        copy = pltpu.make_async_remote_copy(
+            src_ref=src, dst_ref=dst, send_sem=send_sem.at[at], recv_sem=recv_sem.at[at],
+            device_id=where, device_id_type=MESH,
+        )
+        copy.start()
+        sends.append(copy)
+        return copy
+
+    def at_sec(index):
+        return {"section": index}
+
+    def at_tp(index):
+        return {"tp": index}
+
+    tps = [lax.rem(tp + step, 4) for step in range(1, 4)]
+    barrier = pltpu.get_barrier_semaphore()
+    for where in [at_sec(sib), at_sec(cross), at_sec(diag)] + [at_tp(index) for index in tps]:
+        pl.semaphore_signal(barrier, inc=1, device_id=where, device_id_type=MESH)
+    pl.semaphore_wait(barrier, 6)
+
+    others = (sib, cross, diag)
+    got_pack = [send(pack_ref, pack_all.at[sec], at_sec(index)) for index in others]
+    got_pool = [send(pool_ref, pool_sec.at[slot], at_sec(index)) for slot, index in enumerate(others)]
+    pack_all[sec] = pack_ref[...]
+    noise_all[sec] = noise_ref[...]
+    for copy in got_pool:
+        copy.wait_recv()
+    pool_sum[...] = (pool_ref[...] + pool_sec[0]) + (pool_sec[1] + pool_sec[2])
+    got_pool = [send(pool_sum, pool_tp.at[slot], at_tp(index)) for slot, index in enumerate(tps)]
+    for copy in got_pack:
+        copy.wait_recv()
+    for block in range(4):
+        rows = pl.ds(block * tok, tok)
+        packed = pack_all[block]
+        lane = lax.broadcasted_iota(jnp.int32, (tok, 128), 1)
+        lane = jnp.where(lane >= 64, lane - 64, lane).astype(jnp.float32)
+        wide = packed.astype(jnp.float32)
+        row_hot[rows, :] = jnp.where(lane == wide[:, 64:65], 1.0, 0.0).astype(jnp.bfloat16)
+        col_hot[rows, :] = jnp.where(lane == wide[:, 65:66], 1.0, 0.0).astype(jnp.bfloat16)
+        zin[rows, :] = packed[:, :64]
+    for copy in got_pool:
+        copy.wait_recv()
+    pooled = (pool_sum[...] + pool_tp[0]) + (pool_tp[1] + pool_tp[2])
+    pool_sum_all = pool_sec.at[0]
+    pool_sum_all[...] = pooled
+
+    def tiles(start, size, body):
+        @pl.loop(0, size // tile)
+        def _(index):
+            body(pl.ds(pl.multiple_of(start + index * tile, tile), tile))
+
+    def place(rows):
+        for part in range(4):
+            hot = row_hot if part < 2 else col_hot
+            cond[part, rows, :] = dot(hot[rows, :], table_ref[part % 2]) + pool_sum_all[part : part + 1, :]
+
+    tiles(0, total, place)
+
+    def embed(net):
+        when = 0 if net == 0 else 1
+
+        def body(rows):
+            latent = zin[rows, :]
+            squares = jnp.zeros((tile, 1), jnp.float32)
+            for part in range(4):
+                values = dot(latent, win_ref[net, part]) + cond[part, rows, :] + time_ref[when, part]
+                squares += jnp.sum(values * values, axis=1, keepdims=True)
+            values = dot(latent, win_ref[net, sec]) + cond[sec, rows, :] + time_ref[when, sec]
+            hid[net, rows, :] = values
+            scale = lax.rsqrt(squares / (4 * feat) + 1e-06)
+            normed[net, rows, :] = (values * scale).astype(jnp.bfloat16)
+
+        tiles(0, total, body)
+
+    def project(net):
+        far = []
+        for start, size in chunks:
+            def body(rows):
+                far_send[net, rows, :] = dot(normed[net, rows, :], wq[net][diag]).astype(jnp.bfloat16)
+
+            tiles(start, size, body)
+            rows = pl.ds(start, size)
+            far.append(send(far_send.at[net, rows], far_recv.at[net, rows], at_sec(sib)))
+        crossed, near = [], []
+        for index, (start, size) in enumerate(chunks):
+            far[index].wait_recv()
+
+            def body(rows):
+                value = dot(normed[net, rows, :], wq[net][cross])
+                cross_send[net, rows, :] = (value + far_recv[net, rows, :].astype(jnp.float32)).astype(jnp.bfloat16)
+
+            tiles(start, size, body)
+            rows = pl.ds(start, size)
+            crossed.append(send(cross_send.at[net, rows], cross_recv.at[net, rows], at_sec(cross)))
+        for start, size in chunks:
+            def body(rows):
+                near_send[net, rows, :] = dot(normed[net, rows, :], wq[net][sib]).astype(jnp.bfloat16)
+
+            tiles(start, size, body)
+            rows = pl.ds(start, size)
+            near.append(send(near_send.at[net, rows], near_recv.at[net, rows], at_sec(sib)))
+
+        def body(rows):
+            own[net, rows, :] = dot(normed[net, rows, :], wq[net][sec])
+
+        tiles(0, total, body)
+        return crossed, near
+
+    def attend(net, pending):
+        crossed, near = pending
+        for index, (start, size) in enumerate(chunks):
+            near[index].wait_recv()
+            crossed[index].wait_recv()
+
+            def body(rows):
+                value = own[net, rows, :] + near_recv[net, rows, :].astype(jnp.float32)
+                value = value + cross_recv[net, rows, :].astype(jnp.float32)
+                qkv[net, rows, :] = value.astype(jnp.bfloat16)
+
+            tiles(start, size, body)
+        direct = []
+        for start, size in chunks:
+            def body(rows):
+                query = qkv[net, rows, 0:128]
+                keys = qkv[net, :, 128:256]
+                values = qkv[net, :, 256:384]
+                low = lax.broadcasted_iota(jnp.int32, (tile, 128), 1) < HD
+                results = []
+                for head in range(2):
+                    kept = jnp.where(low if head == 0 else jnp.logical_not(low), query.astype(jnp.float32), 0.0)
+                    scores = lax.dot_general(
+                        kept.astype(jnp.bfloat16), keys, (((1,), (1,)), ((), ())),
+                        preferred_element_type=jnp.float32,
+                    ) * HD ** (-0.5)
+                    expo = jnp.exp(scores - jnp.max(scores, axis=1, keepdims=True))
+                    sums = jnp.sum(expo, axis=1, keepdims=True)
+                    results.append(dot(expo.astype(jnp.bfloat16), values) / sums)
+                mix[net, sec, rows, :] = jnp.where(low, results[0], results[1]).astype(jnp.bfloat16)
+
+            tiles(start, size, body)
+            rows = pl.ds(start, size)
+            piece = mix.at[net, sec, rows]
+            direct.append((send(piece, piece, at_sec(cross)), send(piece, piece, at_sec(sib))))
+        return direct
+
+    def forward(net, direct):
+        result = []
+        for index, (start, size) in enumerate(chunks):
+            direct[index][0].wait_recv()
+            piece = mix.at[net, cross, pl.ds(start, size)]
+            result.append(send(piece, piece, at_sec(sib)))
+        return result
+
+    def outward(net, direct, passed):
+        for index in range(len(chunks)):
+            direct[index][1].wait_recv()
+            passed[index].wait_recv()
+
+        def term(slot):
+            rows = pl.ds(pl.multiple_of(slot * tok, tok), tok)
+            left = jnp.concatenate([mix[net, index, rows, :] for index in range(4)], axis=1)
+            return lax.dot_general(
+                left, wo[net][...], (((1,), (1,)), ((), ())), preferred_element_type=jnp.float32
+            ).astype(jnp.bfloat16)
+
+        pending = []
+        for step in (2, 1, 3):
+            z_send[net, step - 1] = term(tps[step - 1])
+            pending.append(send(z_send.at[net, step - 1], z_recv.at[net, step - 1], at_tp(tps[step - 1])))
+        z_own[net] = term(tp)
+        return pending
+
+    def finish(net, pending):
+        for copy in pending:
+            copy.wait_recv()
+        rows = pl.ds(pl.multiple_of(tp * tok, tok), tok)
+        summed = z_own[net].astype(jnp.float32)
+        for step in range(3):
+            summed = summed + z_recv[net, step].astype(jnp.float32)
+        after = hid[net, rows, :] + summed
+        squares = jnp.sum(after * after, axis=1, keepdims=True)
+        f_mine[net, :, 0:64] = dot(after.astype(jnp.bfloat16), fin_ref[net, sec])
+        f_mine[net, :, 64:128] = jnp.broadcast_to(squares, (tok, 64))
+        return send(f_mine.at[net], f_sib.at[net], at_sec(sib))
+
+    def pair(net, copy):
+        copy.wait_recv()
+        f_pair[net] = f_mine[net] + f_sib[net]
+        return send(f_pair.at[net], f_cross.at[net], at_sec(cross))
+
+    def scaled(net, copy):
+        copy.wait_recv()
+        summed = f_pair[net] + f_cross[net]
+        value = summed[:, 0:64] * lax.rsqrt(summed[:, 64:128] / (4 * feat) + 1e-06)
+        f_pack[net, tp, :, 0:64] = value[: tok // 2]
+        f_pack[net, tp, :, 64:128] = value[tok // 2 :]
+        piece = f_pack.at[net, tp]
+        return [send(piece, piece, at_tp(index)) for index in tps]
+
+    def collect(net, pending):
+        for copy in pending:
+            copy.wait_recv()
+        for block in range(4):
+            packed = f_pack[net, block]
+            flow[net, pl.ds(block * tok, tok // 2), :] = packed[:, 0:64]
+            flow[net, pl.ds(block * tok + tok // 2, tok // 2), :] = packed[:, 64:128]
+
+    embed(0)
+    pending = project(0)
+    got_noise = [send(noise_ref, noise_all.at[sec], at_sec(index)) for index in others]
+    direct = attend(0, pending)
+    passed = forward(0, direct)
+    pending = outward(0, direct, passed)
+    collect(0, scaled(0, pair(0, finish(0, pending))))
+    for copy in got_noise:
+        copy.wait_recv()
+    moment = when_ref[0:1, 0:64]
+    for block in range(4):
+        rows = pl.ds(block * tok, tok)
+        both = noise_all[block]
+        start = both[:, 0:64] - flow[0, rows, :]
+        clean[rows, :] = start
+        mixed = (1.0 - moment) * start + moment * both[:, 64:128]
+        noisy[rows, :] = mixed
+        zin[rows, :] = mixed.astype(jnp.bfloat16)
+    pending = {}
+    for net in (1, 2):
+        embed(net)
+        pending[net] = project(net)
+    direct = {net: attend(net, pending[net]) for net in (1, 2)}
+    passed = {net: forward(net, direct[net]) for net in (1, 2)}
+    pending = {net: outward(net, direct[net], passed[net]) for net in (1, 2)}
+    pending = {net: finish(net, pending[net]) for net in (1, 2)}
+    pending = {net: pair(net, pending[net]) for net in (1, 2)}
+    pending = {net: scaled(net, pending[net]) for net in (1, 2)}
+    for net in (1, 2):
+        collect(net, pending[net])
+    real = noisy[...] - moment * flow[1]
+    spread = jnp.sum(jnp.abs(clean[...] - real), axis=1, keepdims=True)
+    spread = jnp.sum(spread, axis=0, keepdims=True) / (total * 64) + 1e-05
+    rows = pl.ds(pl.multiple_of(sec * tok, tok), tok)
+    real = noisy[rows, :] - moment * flow[1, rows, :]
+    fake = noisy[rows, :] - moment * flow[2, rows, :]
+    out_ref[...] = (fake - real) / spread
+    for copy in sends:
+        copy.wait_send()
+
+
+def step_call(*operands):
+    tok, feat, total = operands[1].shape[0], operands[0].shape[1], 4 * operands[1].shape[0]
+    f32, bf16 = jnp.float32, jnp.bfloat16
+    shapes = [
+        ((8, feat), f32), ((3, 8, feat), f32), ((3, 8, feat), f32),
+        ((4, tok, 128), bf16), ((4, tok, 128), f32),
+        ((total, 128), bf16), ((total, 128), bf16), ((total, 64), bf16),
+        ((4, total, feat), f32), ((NETS, total, feat), f32), ((NETS, total, feat), bf16),
+    ]
+    shapes += [((NETS, total, 384), bf16)] * 6
+    shapes += [((NETS, total, 384), f32), ((NETS, total, 384), bf16)]
+    shapes += [((NETS, 4, total, 128), bf16), ((NETS, 3, tok, feat), bf16), ((NETS, 3, tok, feat), bf16)]
+    shapes += [((NETS, tok, feat), bf16)] + [((NETS, tok, 128), f32)] * 4
+    shapes += [((NETS, 4, tok // 2, 128), f32), ((NETS, total, 64), f32), ((total, 64), f32), ((total, 64), f32)]
+    count = 3 * 4 + NETS * (6 + 6 + 3 + 2 + 3)
+    return pl.pallas_call(
+        step_kernel,
+        out_shape=jax.ShapeDtypeStruct((tok, 64), f32),
+        in_specs=[pl.BlockSpec(memory_space=pltpu.VMEM)] * len(operands),
+        out_specs=pl.BlockSpec(memory_space=pltpu.VMEM),
+        scratch_shapes=[pltpu.VMEM(shape, kind) for shape, kind in shapes]
+        + [pltpu.SemaphoreType.DMA((count,)), pltpu.SemaphoreType.DMA((count,))],
+        compiler_params=pltpu.CompilerParams(
+            collective_id=0, has_side_effects=True, vmem_limit_bytes=60 * 2**20
+        ),
+    )(*operands)
+
+
+def by_features(
+    student_noise, renoise_noise, patch_slot, renoise_step, prompt_ids, text_table,
+    student_in, student_qkv, student_out, student_final,
+    real_in, real_qkv, real_out, real_final,
+    fake_in, fake_qkv, fake_out, fake_final,
+):
+    f32, bf16 = jnp.float32, jnp.bfloat16
+    quarter = D // 4
+    vocab_local = text_table.shape[0]
+    first_row = lax.axis_index(("section", "tp")) * vocab_local
+    prompt_row = prompt_ids[0] - first_row
+    matches = (prompt_row[:, None] == jnp.arange(vocab_local, dtype=jnp.int32)[None, :]).astype(bf16)
+    counts = jnp.sum(matches.astype(f32), axis=0).astype(bf16)
+    pool = jnp.dot(counts, text_table, preferred_element_type=f32) / prompt_ids.shape[1]
+    pool = jnp.pad(pool.reshape(4, quarter), ((0, 4), (0, 0)))
+    slots = patch_slot[0]
+    places = jnp.stack([slots // GRID_W, slots % GRID_W], axis=1).astype(bf16)
+    pack = jnp.concatenate([student_noise[0].astype(bf16), jnp.pad(places, ((0, 0), (0, 62)))], axis=1)
+    noise = jnp.concatenate([student_noise[0], renoise_noise[0]], axis=1)
+    frequency = jnp.exp(-math.log(10000.0) * jnp.arange(quarter, dtype=f32) / quarter)
+    angle = jnp.arange(64, dtype=f32)[:, None] * frequency[None, :]
+    table = jnp.stack([jnp.sin(angle), jnp.cos(angle)])
+    high = lax.reduce_precision(table, 8, 7)
+    table = jnp.concatenate([high, table - high], axis=1).astype(bf16)
+    moment = renoise_step[0].astype(f32) / 1000.0
+    times = jnp.stack([time_embed(jnp.float32(1.0)), time_embed(moment)]).reshape(2, 4, 1, quarter)
+    w_in = jnp.stack([student_in, real_in, fake_in]).reshape(NETS, 64, 4, quarter).transpose(0, 2, 1, 3)
+    w_final = jnp.stack([student_final, real_final, fake_final]).reshape(NETS, 4, quarter, 64)
+
+    def by_target(weight):
+        return weight.reshape(quarter, 3, 4, 128).transpose(2, 0, 1, 3).reshape(4, quarter, 384)
+
+    result = step_call(
+        pool, pack, noise, table, times, jnp.full((8, 128), moment, f32), w_in, w_final,
+        by_target(student_qkv), by_target(real_qkv), by_target(fake_qkv),
+        student_out, real_out, fake_out,
+    )
+    return result[None]
+
+
 def solution(mesh):
     placed = (
         P("rep", "section", None),
@@ -182,6 +537,8 @@
         P("section", "tp"),
         P(),
     )
+    sizes = dict(mesh.shape)
+    small = sizes["section"] == 4 and sizes["tp"] == 4 and sizes["rep"] == 2
     return jax.shard_map(
-        per_device, mesh=mesh, in_specs=placed, out_specs=P("rep", "section", None), check_vma=False
-    )
+        by_features if small else per_device, mesh=mesh, in_specs=placed, out_specs=P("rep", "section", None), check_vma=False
+    )

time: 444 us -> 228 us (0.51)
  waiting for transfers between devices: 211 us -> 0 us
  Pallas kernels: 0 us -> 179 us
  blocking collectives: 137 us -> 0 us
  matrix products: 53.1 us -> 5.28 us
  local copies, waits for them, and re-layouts: 10.8 us -> 34.9 us
  between operations: 15.2 us -> 0.92 us
  other arithmetic: 15.8 us -> 7.71 us
    pallas_call x0 -> x1, Pallas kernels: none -> 179 us  [step_call(): pl.pallas_call(step_kernel, out_shape=jax.ShapeDtypeStruct((tok, 64), f32...]
    psum x2 -> x0, waiting for transfers between devices: 123 us -> none  [networks(): lax.psum(group_terms.astype(jnp.bfloat16), 'tp').astype(jnp.float32)]
    all_gather x6 -> x0, waiting for transfers between devices: 84.7 us -> none  [the longest x3 73.1 us: networks(): lax.all_gather(w_qkv, 'section', axis=0, tiled=True)]
    psum x2 -> x0, blocking collectives: 71.7 us -> none  [the longest x1 64.6 us: per_device(): pooled = lax.psum(partial_pool, ('section', 'tp')) / prompt_ids.shape[1]]
    all_gather x6 -> x0, blocking collectives: 65.5 us -> none  [the longest x3 36 us: networks(): value_block = lax.all_gather(values_local, 'section', axis=1, tiled=True)]
    dot_general x19 -> x1, matrix products: 53.1 us -> 5.28 us  [by_features(): jnp.dot(counts, text_table, preferred_element_type=f32)]
    reshape x0 -> x10, local copies, waits for them, and re-layouts: none -> 28.9 us  [the longest x9 28.9 us: by_target(): weight.reshape(quarter, 3, 4, 128).transpose(2, 0, 1, 3)]
    reduce_sum x7 -> x1, other arithmetic: 10.1 us -> 0.36 us  [by_features(): counts = jnp.sum(matches.astype(f32), axis=0).astype(bf16)]
  transfers between devices with their start and end apart: 8 -> 0, of which waited for: 5 -> 0; matrix products, arithmetic and copies ran while one was open for 15% -> 0% of each run, Pallas kernels for 0% -> 0%
where the time goes in v1:
time: 228 us
  Pallas kernels  179 us (79%)
  local copies, waits for them, and re-layouts  34.9 us (15%)
  other arithmetic  7.71 us (3%)
  matrix products  5.28 us (2%)
    pallas_call x1, Pallas kernels, step_call(): pl.pallas_call(step_kernel, out_shape=jax.ShapeDtypeStruct((tok, 64), f32...  179 us
    reshape x9, local copies, waits for them, and re-layouts, by_target(): weight.reshape(quarter, 3, 4, 128).transpose(2, 0, 1, 3)  28.9 us
    dot_general x1, matrix products, by_features(): jnp.dot(counts, text_table, preferred_element_type=f32)  5.28 us

profile of v1, /device:TPU:0, one launch (start us, length us, event | category | flops | bytes accessed | tf_op | source)
XLA Modules:
  0.0 227.8 jit_solution(2412497988357430074)
XLA Ops:
  0.0 0.6 fusion.4
  0.7 0.8 pad_maximum_fusion.2.table_ref
  2.1 0.1 fusion.11
  2.2 0.1 pad_maximum_fusion.6
  2.2 0.1 stack.47
  2.3 0.1 fusion.9
  2.4 0.1 pad_maximum_fusion.5
  2.5 0.1 stack.46
  2.6 0.6 pad_maximum_fusion.4.time_ref
  3.2 0.7 fusion.14
  3.9 0.1 copy.64
  4.1 0.1 copy.63
  4.2 0.7 fusion.6.pack_ref
  4.9 0.4 fusion.1
  5.3 0.0 copy-start.8
  5.3 0.0 copy-start
  5.3 5.3 %convolution_reduce_fusion = f32[2432]{0:T(1024)S(1)} fusion(bf16[2000,1]{0,1:T(2,128)(2,1)S(1)} %reshape.222, bf16[2000,2432]{1,0:T(8,128)(2,1)} %param.23), kind=kOutput, calls=%fused_computation.3 | convolution fusion | flops 9728000 | bytes 9741728 | tf_op jit(solution)/shard_map/dot_general | solution.py:492
  10.6 0.1 reshape.215
  10.7 0.6 pad.8.pool_ref
  11.3 0.1 copy.65
  11.4 0.7 pad_maximum_fusion.3.noise_ref
  12.1 0.6 broadcast_in_dim.4.when_ref
  12.7 2.0 reshape.216
  14.7 3.8 %copy.72 = bf16[608,3,4,128]{0,3,1,2:T(8,128)(2,1)S(1)} copy(bf16[608,3,4,128]{3,2,0,1:T(4,128)(2,1)} %reshape.216) | data formatting | bytes 3735552 | tf_op jit(solution)/shard_map/reshape | solution.py:509
  18.5 2.3 %copy.75.wq0_ref = bf16[4,608,384]{2,1,0:T(8,128)(2,1)} copy(bf16[4,608,384]{1,2,0:T(8,128)(2,1)S(1)} %bitcast.42) | data formatting | bytes 3735552 | tf_op jit(solution)/shard_map/reshape | solution.py:509
  20.8 4.2 %reshape.218 = bf16[608,3,4,128]{3,2,0,1:T(4,128)(2,1)} reshape(bf16[608,3,512]{2,0,1:T(8,128)(2,1)} %param.29) | data formatting | bytes 3735552 | tf_op jit(solution)/shard_map/reshape | solution.py:509
  25.0 3.8 %copy.73 = bf16[608,3,4,128]{0,3,1,2:T(8,128)(2,1)S(1)} copy(bf16[608,3,4,128]{3,2,0,1:T(4,128)(2,1)} %reshape.218) | data formatting | bytes 3735552 | tf_op jit(solution)/shard_map/reshape | solution.py:509
  28.8 2.3 %copy.76.wq1_ref = bf16[4,608,384]{2,1,0:T(8,128)(2,1)} copy(bf16[4,608,384]{1,2,0:T(8,128)(2,1)S(1)} %bitcast.43) | data formatting | bytes 3735552 | tf_op jit(solution)/shard_map/reshape | solution.py:509
  31.2 4.3 %reshape.220 = bf16[608,3,4,128]{3,2,0,1:T(4,128)(2,1)} reshape(bf16[608,3,512]{2,0,1:T(8,128)(2,1)} %param.33) | data formatting | bytes 3735552 | tf_op jit(solution)/shard_map/reshape | solution.py:509
  35.4 3.8 %copy.74 = bf16[608,3,4,128]{0,3,1,2:T(8,128)(2,1)S(1)} copy(bf16[608,3,4,128]{3,2,0,1:T(4,128)(2,1)} %reshape.220) | data formatting | bytes 3735552 | tf_op jit(solution)/shard_map/reshape | solution.py:509
  39.2 0.0 copy-start.1
  39.2 0.0 copy-start.2
  39.2 2.4 %copy.77.wq2_ref = bf16[4,608,384]{2,1,0:T(8,128)(2,1)} copy(bf16[4,608,384]{1,2,0:T(8,128)(2,1)S(1)} %bitcast.44) | data formatting | bytes 3735552 | tf_op jit(solution)/shard_map/reshape | solution.py:509
  41.6 0.3 copy.69
  42.0 0.3 copy.70
  42.3 0.3 copy-done.3
  42.6 0.3 copy.71
  42.9 0.0 copy-start.4
  42.9 0.0 copy-start.5
  42.9 1.7 pad_maximum_fusion.fin_ref
  44.7 0.4 stack.49
  45.1 0.0 copy-done.5
  45.1 0.4 stack.50
  45.5 0.1 copy-done.6
  45.6 0.4 stack.51
  46.0 1.2 maximum_bitcast_fusion.win_ref
  47.2 179.0 %shard_map.172 = f32[192,64]{1,0:T(8,128)} custom-call(f32[8,608]{1,0:T(8,128)} %pad.8.pool_ref, bf16[192,128]{1,0:T(8,128)(2,1)} %fusion.6.pack_ref, f32[192,128]{1,0:T(8,128)} %pad_maximum_fusion.3.noise_ref, bf16[2,128,608]{2,1,0:T(8,128)(2,1)} %pad_maximum_fusion.2.table_ref, f32[2,4,1,608]{3,2,1,0:T(1,128)} %pad_maximum_fusion.4.time_ref, ...), custom_call_target="tpu_custom_call" | custom-call | tf_op jit(solution)/shard_map/pallas_call | solution.py:466
  226.2 1.6 copy.78
  (22 shorter events, 0.2 us)
Async XLA Ops:
  0.0 4.0 %copy-start.7 = (f32[1,192,64]{1,2,0:T(8,128)S(1)}, f32[1,192,64]{1,2,0:T(8,128)}, u32[]{:S(2)}) copy-start(f32[1,192,64]{1,2,0:T(8,128)} %param.18) | copy-start | bytes 147460
  0.0 4.9 %copy-start.9 = (s32[1,256]{1,0:T(1,128)S(1)}, s32[1,256]{1,0:T(1,128)}, u32[]{:S(2)}) copy-start(s32[1,256]{1,0:T(1,128)} %param.22) | copy-start | bytes 3076
  5.3 6.0 %copy-start.8 = (f32[1,192,64]{1,2,0:T(8,128)S(1)}, f32[1,192,64]{1,2,0:T(8,128)}, u32[]{:S(2)}) copy-start(f32[1,192,64]{1,2,0:T(8,128)} %param.19) | copy-start | bytes 147460
  5.3 7.4 %copy-start = (bf16[608,3,512]{2,0,1:T(8,128)(2,1)S(1)}, bf16[608,3,512]{2,0,1:T(8,128)(2,1)}, u32[]{:S(2)}) copy-start(bf16[608,3,512]{2,0,1:T(8,128)(2,1)} %param.25) | copy-start | bytes 5603332
  39.2 2.4 %copy-start.1 = (bf16[2432,64]{0,1:T(8,128)(2,1)S(1)}, bf16[2432,64]{0,1:T(8,128)(2,1)}, u32[]{:S(2)}) copy-start(bf16[2432,64]{0,1:T(8,128)(2,1)} %param.27) | copy-start | bytes 933892
  39.2 2.7 %copy-start.2 = (bf16[2432,64]{0,1:T(8,128)(2,1)S(1)}, bf16[2432,64]{0,1:T(8,128)(2,1)}, u32[]{:S(2)}) copy-start(bf16[2432,64]{0,1:T(8,128)(2,1)} %param.31) | copy-start | bytes 933892
  41.6 1.0 copy-start.3
  42.9 1.7 copy-start.4
  42.9 2.2 copy-start.5
  44.7 1.0 copy-start.6

commit v2 on v1

--- a/solution.py
+++ b/solution.py
@@ -172,16 +172,19 @@
 
 
 def step_kernel(
-    pool_ref, pack_ref, noise_ref, table_ref, time_ref, when_ref, win_ref, fin_ref,
+    pool_ref, pack_ref, noise_ref, table_ref, time_ref, when_ref, win_ref, fin0_ref, fin1_ref, fin2_ref,
     wq0_ref, wq1_ref, wq2_ref, wo0_ref, wo1_ref, wo2_ref,
     out_ref,
     pool_sum, pool_sec, pool_tp, pack_all, noise_all, row_hot, col_hot, zin, cond, hid, normed,
     far_send, far_recv, cross_send, cross_recv, near_send, near_recv, own, qkv,
-    mix, z_send, z_recv, z_own, f_mine, f_sib, f_pair, f_cross, f_pack, flow, clean, noisy,
+    mix, mix_send, wo_all, f_mine, f_sib, f_pair, f_cross, f_pack, flow, clean, noisy,
     send_sem, recv_sem,
 ):
     wq = (wq0_ref, wq1_ref, wq2_ref)
     wo = (wo0_ref, wo1_ref, wo2_ref)
+    fin = (fin0_ref, fin1_ref, fin2_ref)
+    rep = lax.axis_index("rep")
+    peer = 1 - rep
     sec = lax.axis_index("section")
     tp = lax.axis_index("tp")
     core = lax.rem(sec, 2)
@@ -216,19 +219,35 @@
 
     tps = [lax.rem(tp + step, 4) for step in range(1, 4)]
     barrier = pltpu.get_barrier_semaphore()
-    for where in [at_sec(sib), at_sec(cross), at_sec(diag)] + [at_tp(index) for index in tps]:
+    for where in [at_sec(sib), at_sec(cross), at_sec(diag)] + [at_tp(index) for index in tps] + [{"rep": peer}]:
         pl.semaphore_signal(barrier, inc=1, device_id=where, device_id_type=MESH)
-    pl.semaphore_wait(barrier, 6)
+    pl.semaphore_wait(barrier, 7)
 
     others = (sib, cross, diag)
     got_pack = [send(pack_ref, pack_all.at[sec], at_sec(index)) for index in others]
     got_pool = [send(pool_ref, pool_sec.at[slot], at_sec(index)) for slot, index in enumerate(others)]
+    part_rows = feat // 2
+    mine = pl.ds(pl.multiple_of(rep * part_rows, 16), part_rows)
+
+    def spread_weight(net):
+        wo_all[net, tp] = wo[net][...]
+        return [send(wo[net].at[mine], wo_all.at[net, tp, mine], at_tp(tps[step])) for step in (1, 0, 2)]
+
+    def share_weight(net, pending):
+        result = []
+        for copy, step in zip(pending, (2, 1, 3)):
+            copy.wait_recv()
+            piece = wo_all.at[net, lax.rem(tp + 4 - step, 4), mine]
+            result.append(send(piece, piece, {"rep": peer}))
+        return result
+
     pack_all[sec] = pack_ref[...]
     noise_all[sec] = noise_ref[...]
     for copy in got_pool:
         copy.wait_recv()
     pool_sum[...] = (pool_ref[...] + pool_sec[0]) + (pool_sec[1] + pool_sec[2])
     got_pool = [send(pool_sum, pool_tp.at[slot], at_tp(index)) for slot, index in enumerate(tps)]
+    halves = {0: spread_weight(0)}
     for copy in got_pack:
         copy.wait_recv()
     for block in range(4):
@@ -274,11 +293,16 @@
 
         tiles(0, total, body)
 
+    def part_of(net, rows, target):
+        columns = pl.ds(pl.multiple_of(target * 128, 128), 128)
+        left = normed[net, rows, :]
+        return jnp.concatenate([dot(left, wq[net][kind, :, columns]) for kind in range(3)], axis=1)
+
     def project(net):
         far = []
         for start, size in chunks:
             def body(rows):
-                far_send[net, rows, :] = dot(normed[net, rows, :], wq[net][diag]).astype(jnp.bfloat16)
+                far_send[net, rows, :] = part_of(net, rows, diag).astype(jnp.bfloat16)
 
             tiles(start, size, body)
             rows = pl.ds(start, size)
@@ -288,7 +312,7 @@
             far[index].wait_recv()
 
             def body(rows):
-                value = dot(normed[net, rows, :], wq[net][cross])
+                value = part_of(net, rows, cross)
                 cross_send[net, rows, :] = (value + far_recv[net, rows, :].astype(jnp.float32)).astype(jnp.bfloat16)
 
             tiles(start, size, body)
@@ -296,14 +320,14 @@
             crossed.append(send(cross_send.at[net, rows], cross_recv.at[net, rows], at_sec(cross)))
         for start, size in chunks:
             def body(rows):
-                near_send[net, rows, :] = dot(normed[net, rows, :], wq[net][sib]).astype(jnp.bfloat16)
+                near_send[net, rows, :] = part_of(net, rows, sib).astype(jnp.bfloat16)
 
             tiles(start, size, body)
             rows = pl.ds(start, size)
             near.append(send(near_send.at[net, rows], near_recv.at[net, rows], at_sec(sib)))
 
         def body(rows):
-            own[net, rows, :] = dot(normed[net, rows, :], wq[net][sec])
+            own[net, rows, :] = part_of(net, rows, sec)
 
         tiles(0, total, body)
         return crossed, near
@@ -320,68 +344,57 @@
                 qkv[net, rows, :] = value.astype(jnp.bfloat16)
 
             tiles(start, size, body)
-        direct = []
-        for start, size in chunks:
-            def body(rows):
-                query = qkv[net, rows, 0:128]
-                keys = qkv[net, :, 128:256]
-                values = qkv[net, :, 256:384]
-                low = lax.broadcasted_iota(jnp.int32, (tile, 128), 1) < HD
-                results = []
-                for head in range(2):
-                    kept = jnp.where(low if head == 0 else jnp.logical_not(low), query.astype(jnp.float32), 0.0)
-                    scores = lax.dot_general(
-                        kept.astype(jnp.bfloat16), keys, (((1,), (1,)), ((), ())),
-                        preferred_element_type=jnp.float32,
-                    ) * HD ** (-0.5)
-                    expo = jnp.exp(scores - jnp.max(scores, axis=1, keepdims=True))
-                    sums = jnp.sum(expo, axis=1, keepdims=True)
-                    results.append(dot(expo.astype(jnp.bfloat16), values) / sums)
-                mix[net, sec, rows, :] = jnp.where(low, results[0], results[1]).astype(jnp.bfloat16)
-
-            tiles(start, size, body)
-            rows = pl.ds(start, size)
-            piece = mix.at[net, sec, rows]
-            direct.append((send(piece, piece, at_sec(cross)), send(piece, piece, at_sec(sib))))
-        return direct
-
-    def forward(net, direct):
-        result = []
-        for index, (start, size) in enumerate(chunks):
-            direct[index][0].wait_recv()
-            piece = mix.at[net, cross, pl.ds(start, size)]
-            result.append(send(piece, piece, at_sec(sib)))
-        return result
-
-    def outward(net, direct, passed):
-        for index in range(len(chunks)):
-            direct[index][1].wait_recv()
-            passed[index].wait_recv()
-
-        def term(slot):
-            rows = pl.ds(pl.multiple_of(slot * tok, tok), tok)
-            left = jnp.concatenate([mix[net, index, rows, :] for index in range(4)], axis=1)
-            return lax.dot_general(
-                left, wo[net][...], (((1,), (1,)), ((), ())), preferred_element_type=jnp.float32
-            ).astype(jnp.bfloat16)
+        keys = qkv[net, :, 128:256]
+        values = qkv[net, :, 256:384]
+        low = lax.broadcasted_iota(jnp.int32, (tok, 128), 1) < HD
+
+        def block(index):
+            rows = pl.ds(pl.multiple_of(index * tok, tok), tok)
+            query = qkv[net, rows, 0:128].astype(jnp.float32)
+            results = []
+            for head in range(2):
+                kept = jnp.where(low if head == 0 else jnp.logical_not(low), query, 0.0)
+                scores = lax.dot_general(
+                    kept.astype(jnp.bfloat16), keys, (((1,), (1,)), ((), ())),
+                    preferred_element_type=jnp.float32,
+                ) * HD ** (-0.5)
+                expo = jnp.exp(scores - jnp.max(scores, axis=1, keepdims=True))
+                sums = jnp.sum(expo, axis=1, keepdims=True)
+                results.append(dot(expo.astype(jnp.bfloat16), values) / sums)
+            return jnp.where(low, results[0], results[1]).astype(jnp.bfloat16)
 
         pending = []
         for step in (2, 1, 3):
-            z_send[net, step - 1] = term(tps[step - 1])
-            pending.append(send(z_send.at[net, step - 1], z_recv.at[net, step - 1], at_tp(tps[step - 1])))
-        z_own[net] = term(tp)
+            mix_send[net, step - 1] = block(tps[step - 1])
+            pending.append(send(mix_send.at[net, step - 1], mix.at[net, sec, tp], at_tp(tps[step - 1])))
+        mix[net, sec, tp] = block(tp)
         return pending
 
-    def finish(net, pending):
+    def gather(net, pending):
         for copy in pending:
             copy.wait_recv()
+        piece = mix.at[net, sec]
+        return send(piece, piece, at_sec(cross)), send(piece, piece, at_sec(sib))
+
+    def forward(net, direct):
+        direct[0].wait_recv()
+        piece = mix.at[net, cross]
+        return send(piece, piece, at_sec(sib))
+
+    def finish(net, direct, passed, shared):
+        for copy in shared:
+            copy.wait_recv()
+        direct[1].wait_recv()
+        passed.wait_recv()
         rows = pl.ds(pl.multiple_of(tp * tok, tok), tok)
-        summed = z_own[net].astype(jnp.float32)
-        for step in range(3):
-            summed = summed + z_recv[net, step].astype(jnp.float32)
-        after = hid[net, rows, :] + summed
+        after = hid[net, rows, :]
+        for group in range(4):
+            left = jnp.concatenate([mix[net, index, group] for index in range(4)], axis=1)
+            after = after + lax.dot_general(
+                left, wo_all[net, group], (((1,), (1,)), ((), ())), preferred_element_type=jnp.float32
+            )
         squares = jnp.sum(after * after, axis=1, keepdims=True)
-        f_mine[net, :, 0:64] = dot(after.astype(jnp.bfloat16), fin_ref[net, sec])
+        f_mine[net, :, 0:64] = dot(after.astype(jnp.bfloat16), fin[net][sec])
         f_mine[net, :, 64:128] = jnp.broadcast_to(squares, (tok, 64))
         return send(f_mine.at[net], f_sib.at[net], at_sec(sib))
 
@@ -410,10 +423,13 @@
     embed(0)
     pending = project(0)
     got_noise = [send(noise_ref, noise_all.at[sec], at_sec(index)) for index in others]
-    direct = attend(0, pending)
+    moved = attend(0, pending)
+    shared = {0: share_weight(0, halves[0])}
+    direct = gather(0, moved)
+    for net in (1, 2):
+        halves[net] = spread_weight(net)
     passed = forward(0, direct)
-    pending = outward(0, direct, passed)
-    collect(0, scaled(0, pair(0, finish(0, pending))))
+    collect(0, scaled(0, pair(0, finish(0, direct, passed, shared[0]))))
     for copy in got_noise:
         copy.wait_recv()
     moment = when_ref[0:1, 0:64]
@@ -429,10 +445,13 @@
     for net in (1, 2):
         embed(net)
         pending[net] = project(net)
-    direct = {net: attend(net, pending[net]) for net in (1, 2)}
+    moved = {}
+    for net in (1, 2):
+        shared[net] = share_weight(net, halves[net])
+        moved[net] = attend(net, pending[net])
+    direct = {net: gather(net, moved[net]) for net in (1, 2)}
     passed = {net: forward(net, direct[net]) for net in (1, 2)}
-    pending = {net: outward(net, direct[net], passed[net]) for net in (1, 2)}
-    pending = {net: finish(net, pending[net]) for net in (1, 2)}
+    pending = {net: finish(net, direct[net], passed[net], shared[net]) for net in (1, 2)}
     pending = {net: pair(net, pending[net]) for net in (1, 2)}
     pending = {net: scaled(net, pending[net]) for net in (1, 2)}
     for net in (1, 2):
@@ -459,10 +478,10 @@
     ]
     shapes += [((NETS, total, 384), bf16)] * 6
     shapes += [((NETS, total, 384), f32), ((NETS, total, 384), bf16)]
-    shapes += [((NETS, 4, total, 128), bf16), ((NETS, 3, tok, feat), bf16), ((NETS, 3, tok, feat), bf16)]
-    shapes += [((NETS, tok, feat), bf16)] + [((NETS, tok, 128), f32)] * 4
+    shapes += [((NETS, 4, 4, tok, 128), bf16), ((NETS, 3, tok, 128), bf16), ((NETS, 4, feat, 512), bf16)]
+    shapes += [((NETS, tok, 128), f32)] * 4
     shapes += [((NETS, 4, tok // 2, 128), f32), ((NETS, total, 64), f32), ((total, 64), f32), ((total, 64), f32)]
-    count = 3 * 4 + NETS * (6 + 6 + 3 + 2 + 3)
+    count = 3 * 4 + NETS * (6 + 3 + 3 + 6 + 2 + 3)
     return pl.pallas_call(
         step_kernel,
         out_shape=jax.ShapeDtypeStruct((tok, 64), f32),
@@ -503,14 +522,14 @@
     moment = renoise_step[0].astype(f32) / 1000.0
     times = jnp.stack([time_embed(jnp.float32(1.0)), time_embed(moment)]).reshape(2, 4, 1, quarter)
     w_in = jnp.stack([student_in, real_in, fake_in]).reshape(NETS, 64, 4, quarter).transpose(0, 2, 1, 3)
-    w_final = jnp.stack([student_final, real_final, fake_final]).reshape(NETS, 4, quarter, 64)
-
-    def by_target(weight):
-        return weight.reshape(quarter, 3, 4, 128).transpose(2, 0, 1, 3).reshape(4, quarter, 384)
+    w_final = [each.reshape(4, quarter, 64) for each in (student_final, real_final, fake_final)]
+
+    def by_kind(weight):
+        return weight.transpose(1, 0, 2)
 
     result = step_call(
-        pool, pack, noise, table, times, jnp.full((8, 128), moment, f32), w_in, w_final,
-        by_target(student_qkv), by_target(real_qkv), by_target(fake_qkv),
+        pool, pack, noise, table, times, jnp.full((8, 128), moment, f32), w_in, *w_final,
+        by_kind(student_qkv), by_kind(real_qkv), by_kind(fake_qkv),
         student_out, real_out, fake_out,
     )
     return result[None]

time: 228 us -> 211 us (0.925)
  local copies, waits for them, and re-layouts: 34.9 us -> 7.9 us
  Pallas kernels: 179 us -> 190 us
    reshape x9 -> x0, local copies, waits for them, and re-layouts: 28.9 us -> none  [by_target(): weight.reshape(quarter, 3, 4, 128).transpose(2, 0, 1, 3)]
    pallas_call x1, Pallas kernels: 179 us -> 190 us  [step_call(): pl.pallas_call(step_kernel, out_shape=jax.ShapeDtypeStruct((tok, 64), f32...]
where the time goes in v2:
time: 211 us
  Pallas kernels  190 us (90%)
  local copies, waits for them, and re-layouts  7.9 us (4%)
  other arithmetic  6.62 us (3%)
  matrix products  5.18 us (2%)
    pallas_call x1, Pallas kernels, step_call(): pl.pallas_call(step_kernel, out_shape=jax.ShapeDtypeStruct((tok, 64), f32...  190 us
    dot_general x1, matrix products, by_features(): jnp.dot(counts, text_table, preferred_element_type=f32)  5.18 us

profile of v2, /device:TPU:0, one launch (start us, length us, event | category | flops | bytes accessed | tf_op | source)
XLA Modules:
  0.0 210.9 jit_solution(15722528133069559368)
XLA Ops:
  0.7 0.7 broadcast_subtract_fusion
  1.3 0.7 fusion.14
  2.1 0.4 fusion.1
  2.4 0.6 broadcast_in_dim.4.when_ref
  3.0 0.0 copy-start.6
  3.0 0.0 copy-start.7
  3.0 5.2 %convolution_reduce_fusion = f32[2432]{0:T(1024)S(1)} fusion(bf16[2000,1]{0,1:T(2,128)(2,1)S(1)} %reshape.203, bf16[2000,2432]{1,0:T(8,128)(2,1)} %param.23), kind=kOutput, calls=%fused_computation.2 | convolution fusion | flops 9728000 | bytes 9741728 | tf_op jit(solution)/shard_map/dot_general | solution.py:511
  8.2 0.0 copy-start
  8.2 0.1 reshape.199
  8.3 0.6 pad.8.pool_ref
  8.9 0.0 copy-start.1
  8.9 0.1 fusion.11
  9.0 0.1 pad_maximum_fusion.5
  9.1 0.1 stack.35
  9.2 0.1 fusion.9
  9.2 0.1 pad_maximum_fusion.4
  9.3 0.1 stack.34
  9.4 0.6 pad_maximum_fusion.3.time_ref
  10.0 0.1 copy.49
  10.2 0.0 copy-done.6
  10.2 0.1 copy.48
  10.3 0.7 fusion.6.pack_ref
  11.0 0.0 copy-done.7
  11.0 0.1 copy.50
  11.1 0.7 pad_maximum_fusion.2.noise_ref
  11.8 0.0 copy-start.2
  11.8 0.6 fusion.4
  12.5 0.8 pad_maximum_fusion.1.table_ref
  13.3 0.0 copy-done
  13.3 0.4 stack.37
  13.7 0.0 copy-done.1
  13.7 0.4 stack.38
  14.1 0.0 copy-start.3
  14.1 0.0 copy-done.2
  14.1 0.0 copy-start.4
  14.1 0.4 stack.39
  14.5 0.0 copy-start.5
  14.6 1.1 maximum_bitcast_fusion.win_ref
  15.7 0.0 copy-done.3
  15.7 1.1 copy.54
  16.8 0.0 copy-done.4
  16.8 1.1 copy.55
  17.9 0.0 copy-done.5
  17.9 1.1 copy.56
  19.0 190.3 %shard_map.172 = f32[192,64]{1,0:T(8,128)} custom-call(f32[8,608]{1,0:T(8,128)} %pad.8.pool_ref, bf16[192,128]{1,0:T(8,128)(2,1)} %fusion.6.pack_ref, f32[192,128]{1,0:T(8,128)} %pad_maximum_fusion.2.noise_ref, bf16[2,128,608]{2,1,0:T(8,128)(2,1)} %pad_maximum_fusion.1.table_ref, f32[2,4,1,608]{3,2,1,0:T(1,128)} %pad_maximum_fusion.3.time_ref, ...), custom_call_target="tpu_custom_call" | custom-call | tf_op jit(solution)/shard_map/pallas_call | solution.py:485
  209.3 1.6 copy.57
  (10 shorter events, 0.2 us)
Async XLA Ops:
  3.0 7.2 %copy-start.6 = (f32[1,192,64]{1,2,0:T(8,128)S(1)}, f32[1,192,64]{1,2,0:T(8,128)}, u32[]{:S(2)}) copy-start(f32[1,192,64]{1,2,0:T(8,128)} %param.18) | copy-start | bytes 147460
  3.0 8.0 %copy-start.7 = (f32[1,192,64]{1,2,0:T(8,128)S(1)}, f32[1,192,64]{1,2,0:T(8,128)}, u32[]{:S(2)}) copy-start(f32[1,192,64]{1,2,0:T(8,128)} %param.19) | copy-start | bytes 147460
  8.2 5.0 %copy-start = (bf16[64,2432]{1,0:T(8,128)(2,1)S(1)}, bf16[64,2432]{1,0:T(8,128)(2,1)}, u32[]{:S(2)}) copy-start(bf16[64,2432]{1,0:T(8,128)(2,1)} %param.24) | copy-start | bytes 933892
  8.9 4.7 %copy-start.1 = (bf16[64,2432]{1,0:T(8,128)(2,1)S(1)}, bf16[64,2432]{1,0:T(8,128)(2,1)}, u32[]{:S(2)}) copy-start(bf16[64,2432]{1,0:T(8,128)(2,1)} %param.28) | copy-start | bytes 933892
  11.8 2.3 %copy-start.2 = (bf16[64,2432]{1,0:T(8,128)(2,1)S(1)}, bf16[64,2432]{1,0:T(8,128)(2,1)}, u32[]{:S(2)}) copy-start(bf16[64,2432]{1,0:T(8,128)(2,1)} %param.32) | copy-start | bytes 933892
  14.1 1.6 copy-start.3
  14.1 2.7 %copy-start.4 = (bf16[2432,64]{0,1:T(8,128)(2,1)S(1)}, bf16[2432,64]{0,1:T(8,128)(2,1)}, u32[]{:S(2)}) copy-start(bf16[2432,64]{0,1:T(8,128)(2,1)} %param.31) | copy-start | bytes 933892
  14.5 3.3 %copy-start.5 = (bf16[2432,64]{0,1:T(8,128)(2,1)S(1)}, bf16[2432,64]{0,1:T(8,128)(2,1)}, u32[]{:S(2)}) copy-start(bf16[2432,64]{0,1:T(8,128)(2,1)} %param.35) | copy-start | bytes 933892

commit v3 on v1

--- a/solution.py
+++ b/solution.py
@@ -172,12 +172,12 @@
 
 
 def step_kernel(
-    pool_ref, pack_ref, noise_ref, table_ref, time_ref, when_ref, win_ref, fin_ref,
+    pool_ref, pack_ref, noise_ref, table_ref, time_ref, when_ref, win_ref,
     wq0_ref, wq1_ref, wq2_ref, wo0_ref, wo1_ref, wo2_ref,
     out_ref,
     pool_sum, pool_sec, pool_tp, pack_all, noise_all, row_hot, col_hot, zin, cond, hid, normed,
     far_send, far_recv, cross_send, cross_recv, near_send, near_recv, own, qkv,
-    mix, z_send, z_recv, z_own, f_mine, f_sib, f_pair, f_cross, f_pack, flow, clean, noisy,
+    mix, z_send, z_recv, z_own, f_mine, f_sib, f_pair, f_cross, flow_pack, grad_pack, clean, noisy,
     send_sem, recv_sem,
 ):
     wq = (wq0_ref, wq1_ref, wq2_ref)
@@ -274,11 +274,16 @@
 
         tiles(0, total, body)
 
+    def part_of(net, rows, target):
+        columns = pl.ds(pl.multiple_of(target * 128, 128), 128)
+        left = normed[net, rows, :]
+        return jnp.concatenate([dot(left, wq[net][kind, :, columns]) for kind in range(3)], axis=1)
+
     def project(net):
         far = []
         for start, size in chunks:
             def body(rows):
-                far_send[net, rows, :] = dot(normed[net, rows, :], wq[net][diag]).astype(jnp.bfloat16)
+                far_send[net, rows, :] = part_of(net, rows, diag).astype(jnp.bfloat16)
 
             tiles(start, size, body)
             rows = pl.ds(start, size)
@@ -288,7 +293,7 @@
             far[index].wait_recv()
 
             def body(rows):
-                value = dot(normed[net, rows, :], wq[net][cross])
+                value = part_of(net, rows, cross)
                 cross_send[net, rows, :] = (value + far_recv[net, rows, :].astype(jnp.float32)).astype(jnp.bfloat16)
 
             tiles(start, size, body)
@@ -296,14 +301,14 @@
             crossed.append(send(cross_send.at[net, rows], cross_recv.at[net, rows], at_sec(cross)))
         for start, size in chunks:
             def body(rows):
-                near_send[net, rows, :] = dot(normed[net, rows, :], wq[net][sib]).astype(jnp.bfloat16)
+                near_send[net, rows, :] = part_of(net, rows, sib).astype(jnp.bfloat16)
 
             tiles(start, size, body)
             rows = pl.ds(start, size)
             near.append(send(near_send.at[net, rows], near_recv.at[net, rows], at_sec(sib)))
 
         def body(rows):
-            own[net, rows, :] = dot(normed[net, rows, :], wq[net][sec])
+            own[net, rows, :] = part_of(net, rows, sec)
 
         tiles(0, total, body)
         return crossed, near
@@ -381,7 +386,10 @@
             summed = summed + z_recv[net, step].astype(jnp.float32)
         after = hid[net, rows, :] + summed
         squares = jnp.sum(after * after, axis=1, keepdims=True)
-        f_mine[net, :, 0:64] = dot(after.astype(jnp.bfloat16), fin_ref[net, sec])
+        f_mine[net, :, 0:64] = lax.dot_general(
+            after.astype(jnp.bfloat16), win_ref[NETS + net, sec], (((1,), (1,)), ((), ())),
+            preferred_element_type=jnp.float32,
+        )
         f_mine[net, :, 64:128] = jnp.broadcast_to(squares, (tok, 64))
         return send(f_mine.at[net], f_sib.at[net], at_sec(sib))
 
@@ -393,57 +401,69 @@
     def scaled(net, copy):
         copy.wait_recv()
         summed = f_pair[net] + f_cross[net]
-        value = summed[:, 0:64] * lax.rsqrt(summed[:, 64:128] / (4 * feat) + 1e-06)
-        f_pack[net, tp, :, 0:64] = value[: tok // 2]
-        f_pack[net, tp, :, 64:128] = value[tok // 2 :]
-        piece = f_pack.at[net, tp]
-        return [send(piece, piece, at_tp(index)) for index in tps]
-
-    def collect(net, pending):
-        for copy in pending:
-            copy.wait_recv()
-        for block in range(4):
-            packed = f_pack[net, block]
-            flow[net, pl.ds(block * tok, tok // 2), :] = packed[:, 0:64]
-            flow[net, pl.ds(block * tok + tok // 2, tok // 2), :] = packed[:, 64:128]
+        return summed[:, 0:64] * lax.rsqrt(summed[:, 64:128] / (4 * feat) + 1e-06)
+
+    def pack_into(ref, value):
+        ref[tp, 0 : tok // 2, 0:64] = value[: tok // 2]
+        ref[tp, 0 : tok // 2, 64:128] = value[tok // 2 :]
+
+    def to_groups(ref):
+        return [send(ref.at[tp], ref.at[tp], at_tp(index)) for index in tps]
 
     embed(0)
     pending = project(0)
-    got_noise = [send(noise_ref, noise_all.at[sec], at_sec(index)) for index in others]
     direct = attend(0, pending)
     passed = forward(0, direct)
+    got_noise = [send(noise_ref, noise_all.at[sec], at_sec(index)) for index in others]
     pending = outward(0, direct, passed)
-    collect(0, scaled(0, pair(0, finish(0, pending))))
+    pack_into(flow_pack, scaled(0, pair(0, finish(0, pending))))
+    pending = to_groups(flow_pack)
     for copy in got_noise:
+        copy.wait_recv()
+    for copy in pending:
         copy.wait_recv()
     moment = when_ref[0:1, 0:64]
     for block in range(4):
-        rows = pl.ds(block * tok, tok)
         both = noise_all[block]
-        start = both[:, 0:64] - flow[0, rows, :]
-        clean[rows, :] = start
-        mixed = (1.0 - moment) * start + moment * both[:, 64:128]
-        noisy[rows, :] = mixed
-        zin[rows, :] = mixed.astype(jnp.bfloat16)
-    pending = {}
-    for net in (1, 2):
-        embed(net)
-        pending[net] = project(net)
-    direct = {net: attend(net, pending[net]) for net in (1, 2)}
-    passed = {net: forward(net, direct[net]) for net in (1, 2)}
-    pending = {net: outward(net, direct[net], passed[net]) for net in (1, 2)}
-    pending = {net: finish(net, pending[net]) for net in (1, 2)}
-    pending = {net: pair(net, pending[net]) for net in (1, 2)}
-    pending = {net: scaled(net, pending[net]) for net in (1, 2)}
-    for net in (1, 2):
-        collect(net, pending[net])
-    real = noisy[...] - moment * flow[1]
-    spread = jnp.sum(jnp.abs(clean[...] - real), axis=1, keepdims=True)
-    spread = jnp.sum(spread, axis=0, keepdims=True) / (total * 64) + 1e-05
-    rows = pl.ds(pl.multiple_of(sec * tok, tok), tok)
-    real = noisy[rows, :] - moment * flow[1, rows, :]
-    fake = noisy[rows, :] - moment * flow[2, rows, :]
-    out_ref[...] = (fake - real) / spread
+        packed = flow_pack[block]
+        for side in range(2):
+            rows = pl.ds(block * tok + side * (tok // 2), tok // 2)
+            local = slice(side * (tok // 2), (side + 1) * (tok // 2))
+            start = both[local, 0:64] - packed[:, side * 64 : side * 64 + 64]
+            clean[rows, :] = start
+            mixed = (1.0 - moment) * start + moment * both[local, 64:128]
+            noisy[rows, :] = mixed
+            zin[rows, :] = mixed.astype(jnp.bfloat16)
+    embed(1)
+    pending = project(1)
+    embed(2)
+    direct = attend(1, pending)
+    pending = project(2)
+    passed = forward(1, direct)
+    real_terms = outward(1, direct, passed)
+    direct = attend(2, pending)
+    passed = forward(2, direct)
+    fake_terms = outward(2, direct, passed)
+    real_pair = pair(1, finish(1, real_terms))
+    real_flow = scaled(1, real_pair)
+    rows = pl.ds(pl.multiple_of(tp * tok, tok), tok)
+    real = noisy[rows, :] - moment * real_flow
+    spread = jnp.sum(jnp.abs(clean[rows, :] - real), axis=1, keepdims=True)
+    spread = jnp.sum(spread, axis=0, keepdims=True)
+    grad_pack[tp, tok // 2 : tok // 2 + 8, :] = jnp.broadcast_to(spread, (8, 128))
+    fake_flow = scaled(2, pair(2, finish(2, fake_terms)))
+    fake = noisy[rows, :] - moment * fake_flow
+    pack_into(grad_pack, fake - real)
+    pending = to_groups(grad_pack)
+    for copy in pending:
+        copy.wait_recv()
+    spread = jnp.zeros((1, 64), jnp.float32)
+    for block in range(4):
+        spread = spread + grad_pack[block, tok // 2 : tok // 2 + 1, 0:64]
+    spread = spread / (total * 64) + 1e-05
+    packed = grad_pack[sec]
+    out_ref[0 : tok // 2, :] = packed[0 : tok // 2, 0:64] / spread
+    out_ref[tok // 2 : tok, :] = packed[0 : tok // 2, 64:128] / spread
     for copy in sends:
         copy.wait_send()
 
@@ -461,8 +481,8 @@
     shapes += [((NETS, total, 384), f32), ((NETS, total, 384), bf16)]
     shapes += [((NETS, 4, total, 128), bf16), ((NETS, 3, tok, feat), bf16), ((NETS, 3, tok, feat), bf16)]
     shapes += [((NETS, tok, feat), bf16)] + [((NETS, tok, 128), f32)] * 4
-    shapes += [((NETS, 4, tok // 2, 128), f32), ((NETS, total, 64), f32), ((total, 64), f32), ((total, 64), f32)]
-    count = 3 * 4 + NETS * (6 + 6 + 3 + 2 + 3)
+    shapes += [((4, tok // 2, 128), f32), ((4, tok // 2 + 8, 128), f32), ((total, 64), f32), ((total, 64), f32)]
+    count = 3 * 4 + NETS * (6 + 6 + 3 + 2) + 6
     return pl.pallas_call(
         step_kernel,
         out_shape=jax.ShapeDtypeStruct((tok, 64), f32),
@@ -502,15 +522,15 @@
     table = jnp.concatenate([high, table - high], axis=1).astype(bf16)
     moment = renoise_step[0].astype(f32) / 1000.0
     times = jnp.stack([time_embed(jnp.float32(1.0)), time_embed(moment)]).reshape(2, 4, 1, quarter)
-    w_in = jnp.stack([student_in, real_in, fake_in]).reshape(NETS, 64, 4, quarter).transpose(0, 2, 1, 3)
-    w_final = jnp.stack([student_final, real_final, fake_final]).reshape(NETS, 4, quarter, 64)
-
-    def by_target(weight):
-        return weight.reshape(quarter, 3, 4, 128).transpose(2, 0, 1, 3).reshape(4, quarter, 384)
+    thin = jnp.stack([student_in, real_in, fake_in, student_final.T, real_final.T, fake_final.T])
+    thin = thin.reshape(2 * NETS, 64, 4, quarter).transpose(0, 2, 1, 3)
+
+    def by_kind(weight):
+        return weight.transpose(1, 0, 2)
 
     result = step_call(
-        pool, pack, noise, table, times, jnp.full((8, 128), moment, f32), w_in, w_final,
-        by_target(student_qkv), by_target(real_qkv), by_target(fake_qkv),
+        pool, pack, noise, table, times, jnp.full((8, 128), moment, f32), thin,
+        by_kind(student_qkv), by_kind(real_qkv), by_kind(fake_qkv),
         student_out, real_out, fake_out,
     )
     return result[None]

time: 228 us -> 187 us (0.82)
  local copies, waits for them, and re-layouts: 34.9 us -> 8.07 us
  Pallas kernels: 179 us -> 167 us
  other arithmetic: 7.71 us -> 4.85 us
    reshape x9 -> x0, local copies, waits for them, and re-layouts: 28.9 us -> none  [by_target(): weight.reshape(quarter, 3, 4, 128).transpose(2, 0, 1, 3)]
    pallas_call x1, Pallas kernels: 179 us -> 167 us  [step_call(): pl.pallas_call(step_kernel, out_shape=jax.ShapeDtypeStruct((tok, 64), f32...]
where the time goes in v3:
time: 187 us; the launch traced here: 186 us
  Pallas kernels  167 us (89%)
  local copies, waits for them, and re-layouts  8.07 us (4%)
  matrix products  5.19 us (3%)
  other arithmetic  4.85 us (3%)
    pallas_call x1, Pallas kernels, step_call(): pl.pallas_call(step_kernel, out_shape=jax.ShapeDtypeStruct((tok, 64), f32...  167 us
    dot_general x1, matrix products, by_features(): jnp.dot(counts, text_table, preferred_element_type=f32)  5.19 us

profile of v3, /device:TPU:0, one launch (start us, length us, event | category | flops | bytes accessed | tf_op | source)
XLA Modules:
  0.0 186.4 jit_solution(5586698922535886072)
XLA Ops:
  0.0 0.6 fusion.4
  0.7 0.8 pad_maximum_fusion.1.table_ref
  2.1 0.1 fusion.11
  2.2 0.1 pad_maximum_fusion.5
  2.2 0.1 stack.44
  2.3 0.1 fusion.9
  2.4 0.1 pad_maximum_fusion.4
  2.5 0.1 stack.43
  2.6 0.6 pad_maximum_fusion.3.time_ref
  3.2 0.7 fusion.14
  3.9 0.1 copy.46
  4.1 0.9 copy.45
  5.0 0.7 fusion.6.pack_ref
  5.7 0.0 copy-done.8
  5.7 0.4 fusion.1
  6.1 0.0 copy-start.7
  6.1 0.0 copy-start.1
  6.1 5.2 %convolution_reduce_fusion = f32[2432]{0:T(1024)S(1)} fusion(bf16[2000,1]{0,1:T(2,128)(2,1)S(1)} %reshape.197, bf16[2000,2432]{1,0:T(8,128)(2,1)} %param.23), kind=kOutput, calls=%fused_computation.2 | convolution fusion | flops 9728000 | bytes 9741728 | tf_op jit(solution)/shard_map/dot_general | solution.py:512
  11.3 0.0 copy-start.2
  11.3 0.0 copy-start.3
  11.4 0.1 reshape.196
  11.4 0.6 pad.8.pool_ref
  12.1 0.0 copy-done.7
  12.1 0.1 copy.47
  12.1 0.7 pad_maximum_fusion.2.noise_ref
  12.9 0.6 broadcast_in_dim.4.when_ref
  13.5 0.0 copy-done.1
  13.5 0.4 stack.46
  13.9 0.0 copy-done.2
  13.9 0.0 copy-start.5
  13.9 0.4 stack.47
  14.3 0.1 copy_dynamic-update-slice_fusion.4
  14.3 0.0 copy-done.3
  14.4 0.0 copy-start.6
  14.4 0.4 stack.48
  14.7 0.1 copy_dynamic-update-slice_fusion.3
  14.8 0.0 copy-done.4
  14.8 0.4 stack.49
  15.2 0.1 copy_dynamic-update-slice_fusion.2
  15.2 0.0 copy-done.5
  15.2 0.4 stack.50
  15.6 0.1 copy_dynamic-update-slice_fusion.1
  15.7 0.0 copy-done.6
  15.7 0.4 stack.51
  16.1 0.1 copy_dynamic-update-slice_fusion
  16.1 1.3 copy-done
  17.4 167.3 %shard_map.172 = f32[192,64]{1,0:T(8,128)} custom-call(f32[8,608]{1,0:T(8,128)} %pad.8.pool_ref, bf16[192,128]{1,0:T(8,128)(2,1)} %fusion.6.pack_ref, f32[192,128]{1,0:T(8,128)} %pad_maximum_fusion.2.noise_ref, bf16[2,128,608]{2,1,0:T(8,128)(2,1)} %pad_maximum_fusion.1.table_ref, f32[2,4,1,608]{3,2,1,0:T(1,128)} %pad_maximum_fusion.3.time_ref, ...), custom_call_target="tpu_custom_call" | custom-call | tf_op jit(solution)/shard_map/pallas_call | solution.py:486
  184.8 1.6 copy.54
  (12 shorter events, 0.1 us)
Async XLA Ops:
  0.0 5.7 %copy-start.8 = (s32[1,256]{1,0:T(1,128)S(1)}, s32[1,256]{1,0:T(1,128)}, u32[]{:S(2)}) copy-start(s32[1,256]{1,0:T(1,128)} %param.22) | copy-start | bytes 3076
  6.1 5.9 %copy-start.7 = (f32[1,192,64]{1,2,0:T(8,128)S(1)}, f32[1,192,64]{1,2,0:T(8,128)}, u32[]{:S(2)}) copy-start(f32[1,192,64]{1,2,0:T(8,128)} %param.19) | copy-start | bytes 147460
  6.1 7.4 %copy-start.1 = (bf16[64,2432]{1,0:T(8,128)(2,1)S(1)}, bf16[64,2432]{1,0:T(8,128)(2,1)}, u32[]{:S(2)}) copy-start(bf16[64,2432]{1,0:T(8,128)(2,1)} %param.24) | copy-start | bytes 933892
  11.3 2.6 %copy-start.2 = (bf16[64,2432]{1,0:T(8,128)(2,1)S(1)}, bf16[64,2432]{1,0:T(8,128)(2,1)}, u32[]{:S(2)}) copy-start(bf16[64,2432]{1,0:T(8,128)(2,1)} %param.28) | copy-start | bytes 933892
  11.3 3.0 %copy-start.3 = (bf16[64,2432]{1,0:T(8,128)(2,1)S(1)}, bf16[64,2432]{1,0:T(8,128)(2,1)}, u32[]{:S(2)}) copy-start(bf16[64,2432]{1,0:T(8,128)(2,1)} %param.32) | copy-start | bytes 933892
  12.9 1.9 %copy-start.4 = (bf16[2432,64]{0,1:T(8,128)(2,1)S(1)}, bf16[2432,64]{0,1:T(8,128)(2,1)}, u32[]{:S(2)}) copy-start(bf16[2432,64]{0,1:T(8,128)(2,1)} %param.27) | copy-start | bytes 933892
  13.9 1.3 copy-start.5
  14.4 1.3 copy-start.6
  16.1 1.3 copy-start

commit v4 on v3

--- a/solution.py
+++ b/solution.py
@@ -177,11 +177,15 @@
     out_ref,
     pool_sum, pool_sec, pool_tp, pack_all, noise_all, row_hot, col_hot, zin, cond, hid, normed,
     far_send, far_recv, cross_send, cross_recv, near_send, near_recv, own, qkv,
-    mix, z_send, z_recv, z_own, f_mine, f_sib, f_pair, f_cross, flow_pack, grad_pack, clean, noisy,
-    send_sem, recv_sem,
+    mix, z_send, z_recv, z_own, f_mine, f_sib, f_pair, f_cross, flow_pack, grad_pack, clean, noisy, shift, val_ones, wq_all, wo_all,
+    send_sem, recv_sem, stage_sem,
 ):
-    wq = (wq0_ref, wq1_ref, wq2_ref)
-    wo = (wo0_ref, wo1_ref, wo2_ref)
+    staged, staged_out = [], []
+    for net, (source, source_out) in enumerate(((wq0_ref, wo0_ref), (wq1_ref, wo1_ref), (wq2_ref, wo2_ref))):
+        staged.append(pltpu.make_async_copy(source, wq_all.at[net], stage_sem.at[2 * net]))
+        staged_out.append(pltpu.make_async_copy(source_out, wo_all.at[net], stage_sem.at[2 * net + 1]))
+    for copy in staged + staged_out:
+        copy.start()
     sec = lax.axis_index("section")
     tp = lax.axis_index("tp")
     core = lax.rem(sec, 2)
@@ -240,12 +244,6 @@
         row_hot[rows, :] = jnp.where(lane == wide[:, 64:65], 1.0, 0.0).astype(jnp.bfloat16)
         col_hot[rows, :] = jnp.where(lane == wide[:, 65:66], 1.0, 0.0).astype(jnp.bfloat16)
         zin[rows, :] = packed[:, :64]
-    for copy in got_pool:
-        copy.wait_recv()
-    pooled = (pool_sum[...] + pool_tp[0]) + (pool_tp[1] + pool_tp[2])
-    pool_sum_all = pool_sec.at[0]
-    pool_sum_all[...] = pooled
-
     def tiles(start, size, body):
         @pl.loop(0, size // tile)
         def _(index):
@@ -254,9 +252,15 @@
     def place(rows):
         for part in range(4):
             hot = row_hot if part < 2 else col_hot
-            cond[part, rows, :] = dot(hot[rows, :], table_ref[part % 2]) + pool_sum_all[part : part + 1, :]
+            cond[part, rows, :] = dot(hot[rows, :], table_ref[part % 2])
 
     tiles(0, total, place)
+    for copy in got_pool:
+        copy.wait_recv()
+    pooled = (pool_sum[...] + pool_tp[0]) + (pool_tp[1] + pool_tp[2])
+    for part in range(4):
+        for when in range(2):
+            shift[when, part] = pooled[part : part + 1, :] + time_ref[when, part]
 
     def embed(net):
         when = 0 if net == 0 else 1
@@ -265,9 +269,9 @@
             latent = zin[rows, :]
             squares = jnp.zeros((tile, 1), jnp.float32)
             for part in range(4):
-                values = dot(latent, win_ref[net, part]) + cond[part, rows, :] + time_ref[when, part]
+                values = dot(latent, win_ref[net, part]) + cond[part, rows, :] + shift[when, part]
                 squares += jnp.sum(values * values, axis=1, keepdims=True)
-            values = dot(latent, win_ref[net, sec]) + cond[sec, rows, :] + time_ref[when, sec]
+            values = dot(latent, win_ref[net, sec]) + cond[sec, rows, :] + shift[when, sec]
             hid[net, rows, :] = values
             scale = lax.rsqrt(squares / (4 * feat) + 1e-06)
             normed[net, rows, :] = (values * scale).astype(jnp.bfloat16)
@@ -276,16 +280,17 @@
 
     def part_of(net, rows, target):
         columns = pl.ds(pl.multiple_of(target * 128, 128), 128)
-        left = normed[net, rows, :]
-        return jnp.concatenate([dot(left, wq[net][kind, :, columns]) for kind in range(3)], axis=1)
+        right = jnp.concatenate([wq_all[net, kind, :, columns] for kind in range(3)], axis=1)
+        return dot(normed[net, rows, :], right)
 
     def project(net):
+        staged[net].wait()
         far = []
         for start, size in chunks:
             def body(rows):
                 far_send[net, rows, :] = part_of(net, rows, diag).astype(jnp.bfloat16)
 
-            tiles(start, size, body)
+            body(pl.ds(start, size))
             rows = pl.ds(start, size)
             far.append(send(far_send.at[net, rows], far_recv.at[net, rows], at_sec(sib)))
         crossed, near = [], []
@@ -296,21 +301,22 @@
                 value = part_of(net, rows, cross)
                 cross_send[net, rows, :] = (value + far_recv[net, rows, :].astype(jnp.float32)).astype(jnp.bfloat16)
 
-            tiles(start, size, body)
+            body(pl.ds(start, size))
             rows = pl.ds(start, size)
             crossed.append(send(cross_send.at[net, rows], cross_recv.at[net, rows], at_sec(cross)))
         for start, size in chunks:
             def body(rows):
                 near_send[net, rows, :] = part_of(net, rows, sib).astype(jnp.bfloat16)
 
-            tiles(start, size, body)
+            body(pl.ds(start, size))
             rows = pl.ds(start, size)
             near.append(send(near_send.at[net, rows], near_recv.at[net, rows], at_sec(sib)))
 
         def body(rows):
             own[net, rows, :] = part_of(net, rows, sec)
 
-        tiles(0, total, body)
+        for start, size in chunks:
+            body(pl.ds(start, size))
         return crossed, near
 
     def attend(net, pending):
@@ -323,26 +329,28 @@
                 value = own[net, rows, :] + near_recv[net, rows, :].astype(jnp.float32)
                 value = value + cross_recv[net, rows, :].astype(jnp.float32)
                 qkv[net, rows, :] = value.astype(jnp.bfloat16)
+                left = lax.broadcasted_iota(jnp.int32, (tile, 128), 1) < HD
+                val_ones[net, 0, rows, :] = jnp.where(left, value[:, 256:384], 1.0).astype(jnp.bfloat16)
+                val_ones[net, 1, rows, :] = jnp.where(left, 1.0, value[:, 256:384]).astype(jnp.bfloat16)
 
             tiles(start, size, body)
         direct = []
         for start, size in chunks:
             def body(rows):
-                query = qkv[net, rows, 0:128]
+                query = qkv[net, rows, 0:128].astype(jnp.float32) * HD ** (-0.5)
                 keys = qkv[net, :, 128:256]
-                values = qkv[net, :, 256:384]
                 low = lax.broadcasted_iota(jnp.int32, (tile, 128), 1) < HD
                 results = []
                 for head in range(2):
-                    kept = jnp.where(low if head == 0 else jnp.logical_not(low), query.astype(jnp.float32), 0.0)
+                    kept = jnp.where(low if head == 0 else jnp.logical_not(low), query, 0.0)
                     scores = lax.dot_general(
                         kept.astype(jnp.bfloat16), keys, (((1,), (1,)), ((), ())),
                         preferred_element_type=jnp.float32,
-                    ) * HD ** (-0.5)
+                    )
                     expo = jnp.exp(scores - jnp.max(scores, axis=1, keepdims=True))
-                    sums = jnp.sum(expo, axis=1, keepdims=True)
-                    results.append(dot(expo.astype(jnp.bfloat16), values) / sums)
-                mix[net, sec, rows, :] = jnp.where(low, results[0], results[1]).astype(jnp.bfloat16)
+                    results.append(dot(expo.astype(jnp.bfloat16), val_ones[net, head]))
+                sums = pltpu.roll(jnp.where(low, results[1], results[0]), HD, 1)
+                mix[net, sec, rows, :] = (jnp.where(low, results[0], results[1]) / sums).astype(jnp.bfloat16)
 
             tiles(start, size, body)
             rows = pl.ds(start, size)
@@ -367,9 +375,10 @@
             rows = pl.ds(pl.multiple_of(slot * tok, tok), tok)
             left = jnp.concatenate([mix[net, index, rows, :] for index in range(4)], axis=1)
             return lax.dot_general(
-                left, wo[net][...], (((1,), (1,)), ((), ())), preferred_element_type=jnp.float32
+                left, wo_all[net], (((1,), (1,)), ((), ())), preferred_element_type=jnp.float32
             ).astype(jnp.bfloat16)
 
+        staged_out[net].wait()
         pending = []
         for step in (2, 1, 3):
             z_send[net, step - 1] = term(tps[step - 1])
@@ -482,14 +491,17 @@
     shapes += [((NETS, 4, total, 128), bf16), ((NETS, 3, tok, feat), bf16), ((NETS, 3, tok, feat), bf16)]
     shapes += [((NETS, tok, feat), bf16)] + [((NETS, tok, 128), f32)] * 4
     shapes += [((4, tok // 2, 128), f32), ((4, tok // 2 + 8, 128), f32), ((total, 64), f32), ((total, 64), f32)]
+    shapes += [((2, 4, 1, feat), f32), ((NETS, 2, total, 128), bf16)]
+    shapes += [((NETS, 3, feat, 512), bf16), ((NETS, feat, 512), bf16)]
     count = 3 * 4 + NETS * (6 + 6 + 3 + 2) + 6
     return pl.pallas_call(
         step_kernel,
         out_shape=jax.ShapeDtypeStruct((tok, 64), f32),
-        in_specs=[pl.BlockSpec(memory_space=pltpu.VMEM)] * len(operands),
+        in_specs=[pl.BlockSpec(memory_space=pltpu.VMEM)] * (len(operands) - 6)
+        + [pl.BlockSpec(memory_space=pl.ANY)] * 6,
         out_specs=pl.BlockSpec(memory_space=pltpu.VMEM),
         scratch_shapes=[pltpu.VMEM(shape, kind) for shape, kind in shapes]
-        + [pltpu.SemaphoreType.DMA((count,)), pltpu.SemaphoreType.DMA((count,))],
+        + [pltpu.SemaphoreType.DMA((count,)), pltpu.SemaphoreType.DMA((count,)), pltpu.SemaphoreType.DMA((6,))],
         compiler_params=pltpu.CompilerParams(
             collective_id=0, has_side_effects=True, vmem_limit_bytes=60 * 2**20
         ),

time: 187 us -> 180 us (0.963)
  Pallas kernels: 167 us -> 160 us
    pallas_call x1, Pallas kernels: 167 us -> 160 us  [step_call(): pl.pallas_call(step_kernel, out_shape=jax.ShapeDtypeStruct((tok, 64), f32...]
where the time goes in v4:
time: 180 us; the launch traced here: 179 us
  Pallas kernels  160 us (89%)
  local copies, waits for them, and re-layouts  8.07 us (4%)
  matrix products  5.19 us (3%)
  other arithmetic  4.85 us (3%)
    pallas_call x1, Pallas kernels, step_call(): pl.pallas_call(step_kernel, out_shape=jax.ShapeDtypeStruct((tok, 64), f32...  160 us
    dot_general x1, matrix products, by_features(): jnp.dot(counts, text_table, preferred_element_type=f32)  5.19 us

profile of v4, /device:TPU:0, one launch (start us, length us, event | category | flops | bytes accessed | tf_op | source)
XLA Modules:
  0.0 179.5 jit_solution(1838198997990273590)
XLA Ops:
  0.0 0.6 fusion.4
  0.7 0.8 pad_maximum_fusion.1.table_ref
  2.1 0.1 fusion.11
  2.2 0.1 pad_maximum_fusion.5
  2.2 0.1 stack.44
  2.3 0.1 fusion.9
  2.4 0.1 pad_maximum_fusion.4
  2.5 0.1 stack.43
  2.6 0.6 pad_maximum_fusion.3.time_ref
  3.2 0.7 fusion.14
  3.9 0.1 copy.46
  4.1 0.9 copy.45
  5.0 0.7 fusion.6.pack_ref
  5.7 0.0 copy-done.8
  5.7 0.4 fusion.1
  6.1 0.0 copy-start.7
  6.1 0.0 copy-start.1
  6.1 5.2 %convolution_reduce_fusion = f32[2432]{0:T(1024)S(1)} fusion(bf16[2000,1]{0,1:T(2,128)(2,1)S(1)} %reshape.197, bf16[2000,2432]{1,0:T(8,128)(2,1)} %param.23), kind=kOutput, calls=%fused_computation.2 | convolution fusion | flops 9728000 | bytes 9741728 | tf_op jit(solution)/shard_map/dot_general | solution.py:524
  11.3 0.0 copy-start.2
  11.3 0.0 copy-start.3
  11.4 0.1 reshape.196
  11.4 0.6 pad.8.pool_ref
  12.1 0.0 copy-done.7
  12.1 0.1 copy.47
  12.1 0.7 pad_maximum_fusion.2.noise_ref
  12.9 0.6 broadcast_in_dim.4.when_ref
  13.5 0.0 copy-done.1
  13.5 0.4 stack.46
  13.9 0.0 copy-done.2
  13.9 0.0 copy-start.5
  13.9 0.4 stack.47
  14.3 0.1 copy_dynamic-update-slice_fusion.4
  14.3 0.0 copy-done.3
  14.4 0.0 copy-start.6
  14.4 0.4 stack.48
  14.7 0.1 copy_dynamic-update-slice_fusion.3
  14.8 0.0 copy-done.4
  14.8 0.4 stack.49
  15.2 0.1 copy_dynamic-update-slice_fusion.2
  15.2 0.0 copy-done.5
  15.2 0.4 stack.50
  15.6 0.1 copy_dynamic-update-slice_fusion.1
  15.7 0.0 copy-done.6
  15.7 0.4 stack.51
  16.1 0.1 copy_dynamic-update-slice_fusion
  16.1 1.3 copy-done
  17.4 160.4 %shard_map.172 = f32[192,64]{1,0:T(8,128)} custom-call(f32[8,608]{1,0:T(8,128)} %pad.8.pool_ref, bf16[192,128]{1,0:T(8,128)(2,1)} %fusion.6.pack_ref, f32[192,128]{1,0:T(8,128)} %pad_maximum_fusion.2.noise_ref, bf16[2,128,608]{2,1,0:T(8,128)(2,1)} %pad_maximum_fusion.1.table_ref, f32[2,4,1,608]{3,2,1,0:T(1,128)} %pad_maximum_fusion.3.time_ref, ...), custom_call_target="tpu_custom_call" | custom-call | tf_op jit(solution)/shard_map/pallas_call | solution.py:497
  177.9 1.6 copy.54
  (12 shorter events, 0.1 us)
Async XLA Ops:
  0.0 5.7 %copy-start.8 = (s32[1,256]{1,0:T(1,128)S(1)}, s32[1,256]{1,0:T(1,128)}, u32[]{:S(2)}) copy-start(s32[1,256]{1,0:T(1,128)} %param.22) | copy-start | bytes 3076
  6.1 5.9 %copy-start.7 = (f32[1,192,64]{1,2,0:T(8,128)S(1)}, f32[1,192,64]{1,2,0:T(8,128)}, u32[]{:S(2)}) copy-start(f32[1,192,64]{1,2,0:T(8,128)} %param.19) | copy-start | bytes 147460
  6.1 7.4 %copy-start.1 = (bf16[64,2432]{1,0:T(8,128)(2,1)S(1)}, bf16[64,2432]{1,0:T(8,128)(2,1)}, u32[]{:S(2)}) copy-start(bf16[64,2432]{1,0:T(8,128)(2,1)} %param.24) | copy-start | bytes 933892
  11.3 2.6 %copy-start.2 = (bf16[64,2432]{1,0:T(8,128)(2,1)S(1)}, bf16[64,2432]{1,0:T(8,128)(2,1)}, u32[]{:S(2)}) copy-start(bf16[64,2432]{1,0:T(8,128)(2,1)} %param.28) | copy-start | bytes 933892
  11.3 3.0 %copy-start.3 = (bf16[64,2432]{1,0:T(8,128)(2,1)S(1)}, bf16[64,2432]{1,0:T(8,128)(2,1)}, u32[]{:S(2)}) copy-start(bf16[64,2432]{1,0:T(8,128)(2,1)} %param.32) | copy-start | bytes 933892
  12.9 1.9 %copy-start.4 = (bf16[2432,64]{0,1:T(8,128)(2,1)S(1)}, bf16[2432,64]{0,1:T(8,128)(2,1)}, u32[]{:S(2)}) copy-start(bf16[2432,64]{0,1:T(8,128)(2,1)} %param.27) | copy-start | bytes 933892
  13.9 1.3 copy-start.5
  14.4 1.3 copy-start.6
  16.1 1.3 copy-start
